TPU v7x, 128 devices: a whole 4x4x4 slice. The times are simulated.
128 devices in a mesh: series: 4 (over x), tm: 32 (over z, y, core).
Axes of the slice: x: 4, y: 4, z: 4, core: 2. Of those that a mesh axis runs over, the one named last changes fastest.
Arguments:
- raw_values: float32 [4, 4096], P('series', 'tm'), may hold values from -6 to 6
- hours: int32 [4, 4096], P('series', 'tm'), may hold values from 0 to 23
- doc_lengths: int32 [4, 7], P('series'), may hold values from 16 to 4000, as said below
- doc_scale: float32 [4, 7], P('series'), may hold values from 0.5 to 2
- dataset_ids: int32 [4, 7, 1], P('series'), may hold values from 0 to 7
- lag_offsets: int32 [84], replicated, may hold values from 1 to 384, as said below
- w_lag: bfloat16 [87, 144], replicated, may hold values from -0.625 to 0.625
- w_qkv: bfloat16 [2, 144, 432], replicated, may hold values from -0.5 to 0.5
- w_out: bfloat16 [2, 144, 144], replicated, may hold values from -1.5 to 1.5
- w_gate_up: bfloat16 [2, 144, 768], replicated, may hold values from -0.5 to 0.5
- w_down: bfloat16 [2, 384, 144], replicated, may hold values from -0.3125 to 0.3125
- gains: float32 [2, 2, 144], replicated, may hold values from 0.5 to 1.5
- cotangent: float32 [4, 4096, 144], P('series', 'tm'), may hold values from -6 to 6
Outputs:
- activations: float32 [4, 4096, 144], P('series', 'tm')
- raw_grad: float32 [4, 4096], P('series', 'tm')
- scale_mean: float32 [8], replicated
- w_lag_grad: float32 [87, 144], replicated
- w_qkv_grad: float32 [2, 144, 432], replicated
- w_out_grad: float32 [2, 144, 144], replicated
- w_gate_up_grad: float32 [2, 144, 768], replicated
- w_down_grad: float32 [2, 384, 144], replicated
- gains_grad: float32 [2, 2, 144], replicated
Inputs may be any that keep to these rules, and one draw needn't show every extreme that they name: `doc_lengths`: each row holds 3 short series, then one long series, then 3 short series; short ones have 32 // 2 to 32 steps; the row sums to 4096. `lag_offsets`: distinct and rising, the last equal to 384.
All inputs are finite; a program needn't handle non-finite values.
Results may differ from a plain program's by a relative error of at most 0.025.
Values may be sent and summed in bfloat16 or wider, within the bound.
No kernel may reach another device: no remote copies, remote signals or barrier semaphores. Data moves between devices by JAX's collectives and lax.ppermute only.
A program may use at most 192 MiB of HBM per device.

v0:
```python
import math

import jax
import jax.numpy as jnp
import numpy as np
from jax import lax
from jax.experimental import pallas as pl
from jax.experimental.pallas import tpu as pltpu
from jax.sharding import PartitionSpec as P


D = 144
HEADS = 9
HEAD_DIM = 16
FF = 384
LAGS = 84
LAYERS = 2
DATASETS = 8
DOCS = 7
LEN = 4096
MAXLAG = 384
FEATS = 87
EPSILON = 1e-06
MASKED = -1e30
AUG = 176
STAT = AUG - D
LROW = D
DROW = D + 18
BLOCK = 512
BLOCKS = LEN // BLOCK
TILE = 128
TILES = LEN // TILE
STEPS = BLOCKS + 1
SHIFTED = 8
HALF = 64
ROWS = HEADS * HALF
LAGCOLS = 400
EARLY = 103
LATE = 24
WIDE = AUG + HALF
SAFE = 40.0
VMEM = 28 * 2**20

bf16 = jnp.bfloat16
f32 = jnp.float32
HIGH = lax.Precision.HIGHEST


def nn(a, b, precision=None):
    return lax.dot_general(a, b, (((1,), (0,)), ((), ())), precision=precision, preferred_element_type=f32)


def nt(a, b, precision=None):
    return lax.dot_general(a, b, (((1,), (1,)), ((), ())), precision=precision, preferred_element_type=f32)


def tn(a, b, precision=None):
    return lax.dot_general(a, b, (((0,), (0,)), ((), ())), precision=precision, preferred_element_type=f32)


def iota(shape, dim):
    return lax.broadcasted_iota(jnp.int32, shape, dim)


def eye(rows, cols, dtype):
    return (iota((rows, cols), 0) == iota((rows, cols), 1)).astype(dtype)


def column(row, size):
    keep = iota((size, size), 0) == iota((size, size), 1)
    return jnp.sum(jnp.where(keep, row, 0.0), axis=1, keepdims=True)


def pair_of(chip):
    return jnp.where(chip < 8, 2 * chip, TILES - 1 - 2 * chip)


def geometry():
    index = lax.axis_index("tm")
    chip, core = index // 2, index % 2
    tile = pair_of(chip)
    low = jnp.where(core == 0, tile, TILES - 1 - tile)
    return chip, core, low, TILES - 1 - low


def doc_start(places, len_ref):
    start = jnp.zeros_like(places)
    end = jnp.int32(0)
    for d in range(DOCS):
        end = end + len_ref[d]
        start = jnp.where(places >= end, end, start)
    return start


def doc_scale_at(places, len_ref, scale_ref):
    own = jnp.full(places.shape, scale_ref[0], f32)
    end = jnp.int32(0)
    for d in range(1, DOCS):
        end = end + len_ref[d - 1]
        own = jnp.where(places >= end, scale_ref[d], own)
    return own


def own_places(low, high):
    lane = iota((1, TILE), 1)
    return jnp.where(lane < HALF, low, high) * TILE + lane


def half_places(u, tile):
    return iota((HALF, 1), 0) + (tile * TILE + u * HALF)


def rotate(x, cosine, sine):
    cols = x.shape[1]
    parts = x.reshape(HEADS, 2, 8, cols)
    one, two = parts[:, 0], parts[:, 1]
    turned = jnp.stack([one * cosine - two * sine, two * cosine + one * sine], axis=1)
    return turned.reshape(D, cols)


def norm_factor(x):
    return lax.rsqrt(jnp.mean(x * x, axis=0, keepdims=True) + EPSILON)


def norm_back(x, gain, d_normal):
    r = norm_factor(x)
    scaled = d_normal * gain
    inner = jnp.mean(x * scaled, axis=0, keepdims=True)
    d_x = r * scaled - (r * r * r * inner) * x
    return d_x, jnp.sum(d_normal * x * r, axis=1, keepdims=True)


def head_columns(h, *firsts):
    col = iota((1, AUG), 1)
    keep = (col >= h * HEAD_DIM) & (col < (h + 1) * HEAD_DIM)
    for first in firsts:
        keep = keep | (col == first + h)
    return keep


def spread(ref, rows, *firsts):
    zero = jnp.zeros((HALF, AUG), f32)
    for h in range(HEADS):
        keep = head_columns(h, *firsts)
        for u in range(2):
            part = rows[u * HALF : (u + 1) * HALF]
            ref[u, h * HALF : (h + 1) * HALF, 0:AUG] = jnp.where(keep, part, zero).astype(bf16)
    if ref.shape[2] == WIDE:
        unit = eye(HALF, HALF, bf16)
        for h in range(HEADS):
            for u in range(2):
                ref[u, h * HALF : (h + 1) * HALF, AUG:WIDE] = unit


def own_heads(x):
    col = iota((1, D), 1) // HEAD_DIM
    total = jnp.zeros((HALF, D), f32)
    for h in range(HEADS):
        total = jnp.where(col == h, x[h * HALF : (h + 1) * HALF, :D], total)
    return total


def two_parts(x):
    hi = x.astype(bf16)
    return hi, (x - hi.astype(f32)).astype(bf16)


class Tiles:
    def __init__(self, ref):
        self.ref, self.count = ref, 0

    def tile(self, value):
        self.ref[self.count] = value.astype(bf16)
        self.count += 1

    def __call__(self, grads):
        for c in range(grads.shape[1] // TILE):
            for r in range(grads.shape[0] // 16):
                self.tile(grads[16 * r : 16 * (r + 1), c * TILE : (c + 1) * TILE].astype(f32))


class Pairs(Tiles):
    def __init__(self, core, keep_ref, send_ref, rest_ref=None):
        self.core, self.refs, self.rest, self.count, self.even = core, (keep_ref, send_ref), rest_ref, 0, None

    def tile(self, value):
        if self.count == self.refs[0].shape[0]:
            self.rest[0] = value.astype(bf16)
        elif self.even is None:
            self.even = value
        else:
            self.refs[0][self.count] = jnp.where(self.core == 0, self.even, value).astype(bf16)
            self.refs[1][self.count] = jnp.where(self.core == 0, value, self.even).astype(bf16)
            self.even = None
            self.count += 1


def turned(w):
    return tn(w, eye(D, D, bf16)).astype(bf16)


def with_ones(x):
    return jnp.concatenate([x, jnp.ones((STAT, x.shape[1]), bf16)], axis=0)


def key_value_block(normal, w_qkv, rope_ref, k, keys_ref, values_ref):
    mixed = nn(w_qkv[D:], normal)
    at = slice(k * BLOCK, (k + 1) * BLOCK)
    keys = rotate(mixed[:D], rope_ref[0:8, at], rope_ref[8:16, at])
    keys_ref[k] = keys.astype(bf16)
    values_ref[k] = mixed[D:].astype(bf16)
    return head_sizes(keys)


def query_of(normal, w_qkv, cosine, sine):
    turned = rotate(nn(w_qkv[:D], normal), cosine, sine)
    return (turned.astype(bf16).astype(f32) * HEAD_DIM**-0.5).astype(bf16)


def own_rope(rope_ref, low, high):
    def at(tile):
        return rope_ref[:, pl.ds(pl.multiple_of(tile * TILE, TILE), TILE)]

    both = jnp.where(iota((1, TILE), 1) < HALF, at(low), at(high))
    return both[0:8], both[8:16]


def own_tile(ref, low, high):
    lane = iota((1, TILE), 1)

    def at(tile):
        return ref[tile // 4, :, pl.ds(pl.multiple_of((tile % 4) * TILE, TILE), TILE)].astype(f32)

    return jnp.where(lane < HALF, at(low), at(high)).astype(bf16)


def query_bias(u, tile, block, columns, len_ref):
    places = half_places(u, tile)
    start = doc_start(places, len_ref)
    keys = iota((1, columns.stop - columns.start), 1) + (block * BLOCK + columns.start)
    return jnp.where((keys <= places) & (keys >= start), 0.0, MASKED).astype(bf16)


def key_bias(u, tile, block, columns, len_ref):
    keys = half_places(u, tile)
    places = iota((1, columns.stop - columns.start), 1) + (block * BLOCK + columns.start)
    start = doc_start(places, len_ref)
    return jnp.where((keys <= places) & (keys >= start), 0.0, MASKED).astype(bf16)


def scores_of(rows, columns, bias):
    return nn(rows, jnp.concatenate([columns, bias], axis=0))


def run_steps(of_step, low, high, step, unroll=4):
    def several(i, carry):
        for j in range(unroll):
            step(*of_step(i * unroll + j, low, high), slice(0, BLOCK))
        return carry

    lax.fori_loop(0, (STEPS - 1) // unroll, several, 0)


def query_step(s, low, high):
    first = low // 4 + (low % 4 >= 2).astype(jnp.int32)
    late = s >= first
    return late.astype(jnp.int32), jnp.where(late, high, low), s - jnp.where(late, first, 0)


def query_last(low, high):
    late = low % 4 >= 2
    tile = jnp.where(late, high, low)
    return late.astype(jnp.int32), tile, tile // 4, slice(0, BLOCK // 2)


def key_step(s, low, high):
    late_short = (low % 4 < 2).astype(jnp.int32)
    first = low // 4 + 1 - late_short
    late = s >= BLOCKS - first
    block = jnp.where(late, high // 4 + late_short + s - (BLOCKS - first), first + s)
    return late.astype(jnp.int32), jnp.where(late, high, low), block


def key_last(low, high):
    late = low % 4 < 2
    tile = jnp.where(late, high, low)
    return late.astype(jnp.int32), tile, tile // 4, slice(BLOCK // 2, BLOCK)


def head_sizes(x):
    return jnp.sum((x * x).reshape(HEADS, HEAD_DIM, x.shape[1]), axis=1)


def attend(query, k_size, keys_ref, values_ref, len_ref, low, high, qbd, top_ref, acc_ref, q_rows_ref):
    q_rows = nt(eye(TILE, TILE, bf16), query)
    q_rows_ref[...] = q_rows.astype(bf16)
    spread(qbd, jnp.concatenate([q_rows, jnp.zeros((TILE, STAT), f32)], axis=1))
    q_size = jnp.max(head_sizes(query.astype(f32)), axis=1, keepdims=True)
    k_size = jnp.max(k_size, axis=1, keepdims=True)
    acc_ref[...] = jnp.zeros(acc_ref.shape, f32)
    safe = jnp.max(q_size * k_size) <= SAFE * SAFE

    @pl.when(safe)
    def _():
        top_ref[...] = jnp.zeros(top_ref.shape, f32)

        def step(u, tile, block, at):
            scores = scores_of(qbd[u], with_ones(keys_ref[block, :, at]), query_bias(u, tile, block, at, len_ref))
            acc_ref[u] = acc_ref[u] + nt(jnp.exp(scores).astype(bf16), with_ones(values_ref[block, :, at]))

        run_steps(query_step, low, high, step)
        step(*query_last(low, high))

    @pl.when(jnp.logical_not(safe))
    def _():
        top_ref[...] = jnp.full(top_ref.shape, MASKED, f32)

        def step(s, carry):
            h, s = s % HEADS, s // HEADS
            first = low // 4 + 1
            late = s >= first
            u, tile, block = late.astype(jnp.int32), jnp.where(late, high, low), s - jnp.where(late, first, 0)
            rows = pl.ds(pl.multiple_of(h * HALF, HALF), HALF)
            bias = query_bias(u, tile, block, slice(0, BLOCK), len_ref)
            scores = scores_of(qbd[u, rows], with_ones(keys_ref[block]), bias)
            old = top_ref[u, rows]
            new = jnp.maximum(old, jnp.max(scores, axis=1, keepdims=True))
            probs = jnp.exp(scores - new)
            acc_ref[u, rows] = acc_ref[u, rows] * jnp.exp(old - new) + nt(probs.astype(bf16), with_ones(values_ref[block]))
            top_ref[u, rows] = new
            return carry

        lax.fori_loop(0, STEPS * HEADS, step, 0)

    attended, stats = [], []
    lane = iota((1, STAT), 1)
    for u in range(2):
        acc = acc_ref[u]
        total = acc[:, D : D + 1]
        attended.append(own_heads(acc[:, :D] / total))
        parts = two_parts(-(top_ref[u] + jnp.log(total)))
        stat = jnp.zeros((HALF, STAT), f32)
        for j in range(2):
            part = parts[j].astype(f32)
            for h in range(HEADS):
                stat = jnp.where(lane == 9 * j + h, part[h * HALF : (h + 1) * HALF], stat)
        stats.append(stat)
    att_rows = jnp.concatenate(attended, axis=0).astype(bf16)
    stat_rows = jnp.concatenate(stats, axis=0).astype(bf16)
    return nt(eye(D, D, bf16), att_rows).astype(bf16), nt(eye(STAT, STAT, bf16), stat_rows).astype(bf16)


def feed_forward(resid, attended, w_out, w_gate_up, w_down, gain):
    mid = resid + nn(w_out, attended)
    normal = (mid * norm_factor(mid) * gain).astype(bf16)
    gate_up = nn(w_gate_up, normal)
    gate = gate_up[:FF]
    hidden = (gate * jax.nn.sigmoid(gate) * gate_up[FF:]).astype(bf16)
    return mid, normal, gate_up, hidden, mid + nn(w_down, hidden)


def feed_back(grad, attended, mid, gate_up, w_out, w_gate_up, w_down, gain, stat, low_refs, traffic):
    d_out_ref, d_gate_up_ref, d_branch_ref, hidden_ref, normal_ref = low_refs
    d_out = grad.astype(bf16)
    d_hidden = tn(w_down, d_out)
    gate, up = gate_up[:FF], gate_up[FF:]
    sig = jax.nn.sigmoid(gate)
    d_gate = d_hidden * up * (sig * (1.0 + gate * (1.0 - sig)))
    d_up = d_hidden * (gate * sig)
    hidden_ref[...] = (gate * sig * up).astype(bf16)
    normal_ref[...] = (mid * norm_factor(mid) * gain).astype(bf16)
    d_gate_up = jnp.concatenate([d_gate, d_up], axis=0).astype(bf16)
    d_mid, d_gain = norm_back(mid, gain, nn(w_gate_up, d_gate_up))
    grad = grad + d_mid
    d_branch = grad.astype(bf16)
    d_att = nn(w_out, d_branch).astype(bf16)
    d_out_ref[...], d_gate_up_ref[...], d_branch_ref[...] = d_out, d_gate_up, d_branch
    traffic.send(*low_refs)
    product = d_att.astype(f32) * attended.astype(f32)
    delta = -jnp.sum(product.reshape(HEADS, HEAD_DIM, TILE), axis=1)
    delta = jnp.concatenate([delta, jnp.zeros((16 - HEADS, TILE), f32)], axis=0)
    row, col = iota((STAT, 16), 0), iota((STAT, 16), 1)
    stat = stat.astype(f32) + nn(((row == DROW - D + col) & (col < HEADS)).astype(bf16), delta.astype(bf16))
    return grad, jnp.concatenate([d_att, stat.astype(bf16)], axis=0), d_gain


def feed_grads(put, hidden, d_out, normal, d_gate_up, attended, d_branch):
    put(nt(d_out, hidden))
    put(nt(normal, d_gate_up))
    put(nt(attended, d_branch[:TILE]))
    rows = [jnp.zeros((48, TILE), bf16), d_branch[TILE:], jnp.zeros((TILE - 64, TILE), bf16)]
    return nt(attended, jnp.concatenate(rows, axis=0))


def gain_column(gains_ref, which):
    return column(gains_ref[which // 2, which % 2 : which % 2 + 1, :], D)


def first_kernel(
    traffic, features_ref, len_ref, w_dense_ref, gains_ref, w_qkv_ref, rope_ref, chosen_ref, w_out_ref, w_gate_up_ref,
    w_down_ref,
    copies_ref, next_ref, next_resid_ref, keys_ref, values_ref, normal_all, feats_ref, resid_ref, normal_a_ref,
    q_ref, att_ref, stat_ref, mid_ref, gate_up_ref, own_rope_ref,
    series, toeplitz, lagged_ref, qbd, top_ref, acc_ref,
):
    chip, core, low, high = geometry()
    series[0:8, :] = jnp.zeros((8, TILE), f32)
    series[8 : 8 + TILES, :] = features_ref[:, 0, :].astype(bf16).astype(f32)
    toeplitz[:, 0:MAXLAG] = jnp.zeros((TILE, MAXLAG), bf16)

    def shift(m, carry):
        rows = [series[pl.ds(m * SHIFTED + 7 + n, 1), :] for n in range(SHIFTED + 1)]
        window = jnp.broadcast_to(jnp.concatenate(rows, axis=1), (TILE, (SHIFTED + 1) * TILE))
        rolled = pltpu.roll(window, 1, 1, stride=1, stride_axis=0)
        at = pl.multiple_of(m * SHIFTED * TILE + MAXLAG, TILE)
        toeplitz[:, pl.ds(at, SHIFTED * TILE)] = rolled[:, TILE:].astype(bf16)
        return carry

    lax.fori_loop(0, TILES // SHIFTED, shift, 0)

    def others(tiles):
        rows = jnp.concatenate([features_ref[t] for t in tiles], axis=1)
        return jnp.concatenate([rows, jnp.zeros_like(rows)], axis=0).astype(bf16)

    traffic.ready(5)
    w_dense = w_dense_ref[...]
    gain_a, gain_b = gain_column(gains_ref, 0), gain_column(gains_ref, 1)
    w_qkv = w_qkv_ref[...]
    lag_rows = iota((TILE, 1), 0) + 1
    k_size = jnp.zeros((HEADS, BLOCK), f32)
    for k in range(BLOCKS):
        place = iota((1, BLOCK), 1) + k * BLOCK
        start = doc_start(place, len_ref)
        parts = []
        for b in range(3):
            at = MAXLAG + k * BLOCK - b * TILE
            lagged = toeplitz[:, at : at + BLOCK]
            if k in (0, BLOCKS - 1):
                valid = place - (lag_rows + b * TILE) >= start
                lagged = jnp.where(valid, lagged.astype(f32), 0.0).astype(bf16)
            parts.append(lagged)
        parts.append(others(range(4 * k, 4 * k + 4)))
        resid = nn(w_dense, jnp.concatenate(parts, axis=0))
        normal = (resid * norm_factor(resid) * gain_a).astype(bf16)
        normal_all[k] = normal
        k_size = jnp.maximum(k_size, key_value_block(normal, w_qkv, rope_ref, k, keys_ref, values_ref))

    cosine, sine = own_rope(rope_ref, low, high)
    own_rope_ref[0:8], own_rope_ref[8:16] = cosine, sine
    traffic.send(keys_ref, values_ref, normal_all, own_rope_ref)

    place = own_places(low, high)
    start = doc_start(place, len_ref)
    lane = iota((1, TILE), 1)

    def tile_of(ref, tile):
        return ref[:, pl.ds(pl.multiple_of(tile * TILE, TILE), TILE)].astype(f32)

    for b in range(3):
        lagged = jnp.where(lane < HALF, tile_of(toeplitz, low + 3 - b), tile_of(toeplitz, high + 3 - b))
        valid = place - (lag_rows + b * TILE) >= start
        lagged_ref[b * TILE : (b + 1) * TILE, :] = jnp.where(valid, lagged, 0.0).astype(bf16)
    lagged_ref[MAXLAG:, :] = jnp.where(lane < HALF, others([low]).astype(f32), others([high]).astype(f32)).astype(bf16)
    lagged = lagged_ref[...]
    resid = nn(w_dense, lagged)
    resid_ref[...] = resid
    normal = (resid * norm_factor(resid) * gain_a).astype(bf16)
    normal_a_ref[...] = normal
    traffic.send(resid_ref, normal_a_ref)
    query = query_of(normal, w_qkv, cosine, sine)
    attended, stat_ref[...] = attend(query, k_size, keys_ref, values_ref, len_ref, low, high, qbd, top_ref, acc_ref, q_ref)
    att_ref[...] = attended
    traffic.send(q_ref, att_ref, stat_ref)
    traffic.ready()
    feats_ref[...] = nn(chosen_ref[...], lagged).astype(bf16)
    mid, _, gate_up, _, resid = feed_forward(resid, attended, w_out_ref[...], w_gate_up_ref[...], w_down_ref[...], gain_b)
    mid_ref[...], gate_up_ref[...] = mid, gate_up
    traffic.send(mid_ref, gate_up_ref, feats_ref)
    next_resid_ref[...] = resid
    normal = (resid * norm_factor(resid) * gain_column(gains_ref, 2)).astype(bf16)
    next_ref[...] = normal
    copies_ref[...] = jnp.broadcast_to(normal[None], copies_ref.shape)


def natural_tiles(own_ref, other_ref, put):
    _, core, _, _ = geometry()
    mine = (iota((1, TILE), 1) < HALF) == (core == 0)
    for chip in range(TILES // 2):
        tile = 2 * chip if chip < 8 else TILES - 1 - 2 * chip
        first, second = jnp.where(core == 0, chip, 15 - chip), jnp.where(core == 0, 15 - chip, chip)
        own, other = own_ref[first].astype(f32), other_ref[second].astype(f32)
        for t, value in ((tile, jnp.where(mine, own, other)), (TILES - 1 - tile, jnp.where(mine, other, own))):
            put(t // 4, slice(t % 4 * TILE, (t % 4 + 1) * TILE), value.astype(bf16))


def second_kernel(
    traffic, own_ref, other_ref, cot_own_ref, cot_other_ref, len_ref, turned_qkv_ref, rope_ref, normal_ref, own_rope_ref, resid_in_ref,
    turned_out_ref, turned_gate_up_ref, w_out_ref, w_gate_up_ref, w_down_ref, gains_ref,
    copies_ref, payload_ref, act_ref, keys_ref, values_ref, normal_all, q_ref, grad_ref, att_ref, d_gain_ref,
    d_out_ref, d_gate_up_ref, d_branch_ref, hidden_ref, normal_b_ref,
    qbd, top_ref, acc_ref,
):
    chip, core, low, high = geometry()

    def put(block, columns, value):
        normal_all[block, :, columns] = value

    natural_tiles(own_ref, other_ref, put)
    traffic.send(normal_all)
    traffic.ready(5)
    w_qkv = turned_qkv_ref[...]
    k_size = jnp.zeros((HEADS, BLOCK), f32)
    for k in range(BLOCKS):
        k_size = jnp.maximum(k_size, key_value_block(normal_all[k], w_qkv, rope_ref, k, keys_ref, values_ref))
    traffic.send(keys_ref, values_ref)
    query = query_of(normal_ref[...], w_qkv, own_rope_ref[0:8], own_rope_ref[8:16])
    attended, stat = attend(query, k_size, keys_ref, values_ref, len_ref, low, high, qbd, top_ref, acc_ref, q_ref)
    traffic.ready()
    gain = gain_column(gains_ref, 3)
    w_out, w_gate_up, w_down = w_out_ref[...], w_gate_up_ref[...], w_down_ref[...]
    mid, _, gate_up, _, out = feed_forward(
        resid_in_ref[...], attended, turned_out_ref[...], turned_gate_up_ref[...], w_down, gain
    )
    act_ref[...] = out
    att_ref[...] = attended
    traffic.send(act_ref, att_ref, q_ref)
    grad = tile_halves(cot_own_ref[...].astype(f32), cot_other_ref[...].astype(f32))
    low_refs = (d_out_ref, d_gate_up_ref, d_branch_ref, hidden_ref, normal_b_ref)
    grad, payload, d_gain_ref[...] = feed_back(grad, attended, mid, gate_up, w_out, w_gate_up, w_down, gain, stat, low_refs, traffic)
    grad_ref[...] = grad
    payload_ref[...] = payload
    copies_ref[...] = jnp.broadcast_to(payload[None], copies_ref.shape)


def query_back(
    traffic, count, payload_ref, q_ref, len_ref, own_rope_ref, rope_ref, keys_ref, values_ref, normal_all, w_qkv_ref, dq_ref, qall_ref,
    k_rows_ref, v_rows_ref, qbd, dbd, acc_ref,
):
    chip, core, low, high = geometry()
    traffic.ready(count)
    unit = eye(TILE, TILE, bf16)
    rows = nt(unit, payload_ref[...])
    spread(qbd, jnp.concatenate([q_ref[...].astype(f32), rows[:, D:]], axis=1), LROW, LROW + 9)
    spread(dbd, rows, DROW)
    k_rows_ref[...] = nt(unit, own_tile(keys_ref, low, high)).astype(bf16)
    v_rows_ref[...] = nt(unit, own_tile(values_ref, low, high)).astype(bf16)
    w_qkv = w_qkv_ref[...]

    def queries(k, carry):
        at = pl.ds(pl.multiple_of(k * BLOCK, BLOCK), BLOCK)
        qall_ref[k] = query_of(normal_all[k], w_qkv, rope_ref[0:8, at], rope_ref[8:16, at])
        return carry

    lax.fori_loop(0, BLOCKS, queries, 0, unroll=2)
    traffic.send(k_rows_ref, v_rows_ref, qall_ref)
    acc_ref[...] = jnp.zeros(acc_ref.shape, f32)

    def step(u, tile, block, at):
        scores = scores_of(qbd[u], with_ones(keys_ref[block, :, at]), query_bias(u, tile, block, at, len_ref))
        d_scores = jnp.exp(scores) * nn(dbd[u], with_ones(values_ref[block, :, at]))
        acc_ref[u] = acc_ref[u] + nt(d_scores.astype(bf16), keys_ref[block, :, at])

    run_steps(query_step, low, high, step, 2)
    step(*query_last(low, high))
    d_query = jnp.concatenate([own_heads(acc_ref[0]), own_heads(acc_ref[1])], axis=0) * HEAD_DIM**-0.5
    dq_ref[...] = rotate(turned_rows(d_query), own_rope_ref[0:8], -own_rope_ref[8:16])


def turned_rows(x):
    hi, lo = two_parts(x)
    unit = eye(D, D, bf16)
    return nt(unit, hi) + nt(unit, lo)


def key_back(traffic, count, own_ref, other_ref, len_ref, qall_ref, k_rows_ref, v_rows_ref, dq_ref, grad_ref, resid_ref, w_qkv_ref, gain,
             own_rope_ref, daug, kbd, vbd, dk_ref, dv_ref):
    chip, core, low, high = geometry()

    def put(block, columns, value):
        daug[block, :, columns] = value

    natural_tiles(own_ref, other_ref, put)
    traffic.ready(count)
    ones = jnp.ones((TILE, STAT), f32)
    spread(kbd, jnp.concatenate([k_rows_ref[...].astype(f32), ones], axis=1), LROW, LROW + 9)
    spread(vbd, jnp.concatenate([v_rows_ref[...].astype(f32), ones], axis=1), DROW)
    dk_ref[...] = jnp.zeros(dk_ref.shape, f32)
    dv_ref[...] = jnp.zeros(dv_ref.shape, f32)

    def step(u, tile, block, at):
        queries = jnp.concatenate([qall_ref[block, :, at], daug[block, D:AUG, at]], axis=0)
        probs = jnp.exp(scores_of(kbd[u], queries, key_bias(u, tile, block, at, len_ref)))
        d_scores = probs * nn(vbd[u], daug[block, :, at])
        dv_ref[u] = dv_ref[u] + nt(probs.astype(bf16), daug[block, :, at])
        dk_ref[u] = dk_ref[u] + nt(d_scores.astype(bf16), qall_ref[block, :, at])

    run_steps(key_step, low, high, step)
    step(*key_last(low, high))
    traffic.ready()
    d_key = turned_rows(jnp.concatenate([own_heads(dk_ref[0]), own_heads(dk_ref[1])], axis=0))
    d_value = nt(eye(D, D, bf16), jnp.concatenate([own_heads(dv_ref[0]), own_heads(dv_ref[1])], axis=0).astype(bf16))
    d_key = rotate(d_key, own_rope_ref[0:8], -own_rope_ref[8:16])
    d_mixed = jnp.concatenate([dq_ref[...], d_key, d_value], axis=0).astype(bf16)
    d_in, d_gain = norm_back(resid_ref[...], gain(), nn(w_qkv_ref[...], d_mixed))
    return grad_ref[...] + d_in, d_mixed, d_gain


def projection_grads(normal, d_mixed):
    tail = nt(normal, jnp.concatenate([d_mixed[MAXLAG:], jnp.zeros((TILE - 48, TILE), bf16)], axis=0))
    return nt(normal, d_mixed[:MAXLAG]), tail


def third_kernel(
    traffic, own_ref, other_ref, len_ref, qall_ref, k_rows_ref, v_rows_ref, dq_ref, grad_in_ref, resid_ref, att_ref, stat_ref, mid_ref,
    gate_up_ref, own_rope_ref, w_qkv_ref, w_out_ref, w_gate_up_ref, w_down_ref, gains_ref,
    copies_ref, payload_ref, grad_ref, d_mixed_ref, d_gain_a_ref, d_gain_b_ref, d_out_ref, d_gate_up_ref, d_branch_ref, hidden_ref,
    normal_b_ref,
    daug, kbd, vbd, dk_ref, dv_ref,
):
    grad, d_mixed_ref[...], d_gain_a_ref[...] = key_back(
        traffic, 4, own_ref, other_ref, len_ref, qall_ref, k_rows_ref, v_rows_ref, dq_ref, grad_in_ref, resid_ref, w_qkv_ref,
        lambda: gain_column(gains_ref, 2), own_rope_ref, daug, kbd, vbd, dk_ref, dv_ref,
    )
    low_refs = (d_out_ref, d_gate_up_ref, d_branch_ref, hidden_ref, normal_b_ref)
    grad, payload, d_gain_b_ref[...] = feed_back(
        grad, att_ref[...], mid_ref[...], gate_up_ref[...], w_out_ref[...], w_gate_up_ref[...], w_down_ref[...], gain_column(gains_ref, 1),
        stat_ref[...], low_refs, traffic,
    )
    grad_ref[...] = grad
    payload_ref[...] = payload
    copies_ref[...] = jnp.broadcast_to(payload[None], copies_ref.shape)


def second_window_kernel(
    traffic, len_ref, hidden_ref, d_out_ref, normal_ref, d_gate_up_ref, att_ref, d_branch_ref, d_gain_ref, payload_ref, q_ref,
    own_rope_ref, rope_ref, keys_ref, values_ref, normal_all, w_qkv_ref,
    pack_ref, tail_ref, dq_ref, qall_ref, k_rows_ref, v_rows_ref, qbd, dbd, acc_ref,
):
    traffic.ready(8)
    tail = feed_grads(
        Tiles(pack_ref), hidden_ref[...], d_out_ref[...], normal_ref[...], d_gate_up_ref[...], att_ref[...], d_branch_ref[...]
    )
    tail_ref[...] = jnp.where(iota((1, TILE), 1) == 99, d_gain_ref[...], tail)
    traffic.send(pack_ref, tail_ref)
    query_back(
        traffic, 16, payload_ref, q_ref, len_ref, own_rope_ref, rope_ref, keys_ref, values_ref, normal_all, w_qkv_ref, dq_ref, qall_ref,
        k_rows_ref, v_rows_ref, qbd, dbd, acc_ref,
    )


def third_window_kernel(
    traffic, len_ref, pack_in_ref, tail_in_ref, normal_a_ref, d_mixed_ref, d_gain_a_ref, hidden_ref, d_out_ref, normal_ref, d_gate_up_ref,
    att_ref, d_branch_ref, d_gain_b_ref, payload_ref, q_ref, own_rope_ref, rope_ref, keys_ref, values_ref, normal_all,
    w_qkv_ref,
    keep_ref, send_ref, rest_ref, tail0_ref, tail1_ref, dq_ref, qall_ref, k_rows_ref, v_rows_ref, qbd, dbd, acc_ref,
):
    traffic.ready(13)
    put = Pairs(lax.axis_index("tm") % 2, keep_ref, send_ref, rest_ref)
    for t in range(pack_in_ref.shape[0]):
        put.tile(pack_in_ref[t].astype(f32))
    head, tail = projection_grads(normal_a_ref[...], d_mixed_ref[...])
    put(head)
    tail0_ref[...] = feed_grads(
        put, hidden_ref[...], d_out_ref[...], normal_ref[...], d_gate_up_ref[...], att_ref[...], d_branch_ref[...]
    )
    lane = iota((1, TILE), 1)
    tail = jnp.where(lane == 98, d_gain_a_ref[...], tail + tail_in_ref[...])
    tail1_ref[...] = jnp.where(lane == 97, d_gain_b_ref[...], tail)
    traffic.send(keep_ref, send_ref, rest_ref, tail0_ref, tail1_ref)
    query_back(
        traffic, 21, payload_ref, q_ref, len_ref, own_rope_ref, rope_ref, keys_ref, values_ref, normal_all, w_qkv_ref, dq_ref, qall_ref,
        k_rows_ref, v_rows_ref, qbd, dbd, acc_ref,
    )


def last_kernel(
    traffic, own_ref, other_ref, len_ref, scale_ref, ids_ref, qall_ref, k_rows_ref, v_rows_ref, dq_ref, grad_in_ref, resid_ref,
    normal_a_ref, tail0_ref, tail1_ref, rest_ref, w_dense_ref, feats_ref, own_rope_ref, w_qkv_ref, gains_ref,
    keep_ref, send_ref, daug, kbd, vbd, dk_ref, dv_ref, raw_ref,
):
    chip, core, low, high = geometry()
    d_first, d_mixed, d_gain = key_back(
        traffic, 6, own_ref, other_ref, len_ref, qall_ref, k_rows_ref, v_rows_ref, dq_ref, grad_in_ref, resid_ref, w_qkv_ref,
        lambda: gain_column(gains_ref, 0), own_rope_ref, daug, kbd, vbd, dk_ref, dv_ref,
    )
    head, tail0 = projection_grads(normal_a_ref[...], d_mixed)
    d_first = d_first.astype(bf16)
    feats = feats_ref[...]
    empty = jnp.zeros((64, TILE), bf16)
    tail0 = tail0 + tail0_ref[...] + nt(d_first, jnp.concatenate([empty, feats[:64]], axis=0))
    tail1 = tail1_ref[...] + nt(d_first, jnp.concatenate([empty, feats[64:], empty[:32]], axis=0))
    lane, row = iota((1, TILE), 1), iota((D, 1), 0)
    tail1 = jnp.where(lane == 96, d_gain, tail1)
    sums, counts = jnp.zeros((D, 1), f32), jnp.zeros((D, 1), f32)
    owner = (lax.axis_index("tm") == 0).astype(f32)
    for d in range(DOCS):
        hit = jnp.where(row == ids_ref[d], owner, 0.0)
        sums, counts = sums + hit * scale_ref[d], counts + hit
    high_part = sums.astype(bf16).astype(f32)
    tail1 = jnp.where(lane == 100, high_part, tail1)
    tail1 = jnp.where(lane == 101, sums - high_part, tail1)
    tail1 = jnp.where(lane == 102, counts, tail1)

    place = own_places(low, high)
    start = doc_start(place, len_ref)
    own = doc_scale_at(place, len_ref, scale_ref)
    flip = (iota((TILE, TILE), 0) + iota((TILE, TILE), 1) == TILE - 1).astype(bf16)
    raw_ref[...] = jnp.zeros(raw_ref.shape, f32)
    lags = TILE - iota((TILE, 1), 0)
    for b in range(3):
        weights = nn(w_dense_ref[:, b * TILE : (b + 1) * TILE], flip).astype(bf16)
        d_lagged = tn(weights, d_first)
        valid = place - (lags + b * TILE) >= start
        d_lagged = jnp.where(valid, d_lagged, 0.0) / own
        for u in range(2):
            half = jnp.where((lane < HALF) == (u == 0), d_lagged, 0.0)
            wide = jnp.concatenate([jnp.zeros((TILE, TILE), f32), half], axis=1)
            rolled = pltpu.roll(wide, TILE, 1, stride=1, stride_axis=0)
            total = jnp.sum(rolled, axis=0, keepdims=True)
            for tile, part in (((low if u == 0 else high) - b + 16, total[:, TILE:]), ((low if u == 0 else high) - b + 15, total[:, :TILE])):
                at = tile % 2, pl.ds(tile // 2, 1)
                raw_ref[at] = raw_ref[at] + part

    put = Pairs(core, keep_ref, send_ref)
    put.tile(rest_ref[0].astype(f32))
    for part in (head, tail0, tail1):
        put(part)
    for k in range(2):
        put.tile(raw_ref[k, 8:24, :])


def summed(in_ref):
    count, rows, _ = in_ref.shape
    total = jnp.zeros((rows, TILE), f32)
    return lax.fori_loop(0, count // 8, lambda i, t: t + jnp.sum(in_ref[pl.ds(i * 8, 8)].astype(f32), axis=0), total)


def pair_sum_kernel(early_ref, early_in_ref, late_ref, late_in_ref, out_ref):
    zero = jnp.zeros((16, TILE), bf16)
    late = late_ref.shape[0] - 1
    series, core = lax.axis_index("series"), lax.axis_index("tm") % 2
    out_ref[:, 32:40, :] = jnp.zeros((64, 8, TILE), bf16)

    def both(ref, in_ref, t):
        return ref[t].astype(f32) + in_ref[t].astype(f32)

    for t in range(128):
        value = zero
        if t < EARLY:
            value = both(early_ref, early_in_ref, t).astype(bf16)
        elif t < EARLY + late:
            value = both(late_ref, late_in_ref, t - EARLY).astype(bf16)
        out_ref[jnp.where(core == 0, t // 2, 63 - t // 2), t % 2 * 16 : t % 2 * 16 + 16, :] = value
    raw = both(late_ref, late_in_ref, late)
    for c in range(16):
        line = jnp.where(iota((8, 1), 0) == 0, raw[c : c + 1], 0.0)
        chip = series * 16 + c
        out_ref[jnp.where(core == 0, chip, 63 - chip), 32:40, :] = line.astype(bf16)


def sum_kernel(in_ref, out_ref, raw_ref):
    total = summed(in_ref)
    out_ref[...] = jnp.broadcast_to(total[:32].astype(bf16)[None], out_ref.shape)
    raw_ref[...] = total[32:33]


def unpack_kernel(own_ref, other_ref, act_in_ref, act_ref, lag_ref, qkv_ref, out_ref, gate_up_ref, down_ref, gains_ref, scale_ref):
    core = lax.axis_index("tm") % 2
    act_ref[...] = act_in_ref[...]

    def tile(t):
        rows = slice(t // 2 % 2 * 16, t // 2 % 2 * 16 + 16)
        first, second = jnp.where(core == 0, t // 4, 63 - t // 4), jnp.where(core == 0, 63 - t // 4, t // 4)
        return jnp.where(core == t % 2, own_ref[first, rows].astype(f32), other_ref[second, rows].astype(f32))

    def columns(first, count):
        return [jnp.concatenate([tile(first + 9 * c + r) for r in range(9)], axis=0) for c in range(count)]

    layers = ((207, 234, 117), (90, 243, 0))
    tails = []
    for layer, (at_qkv, at_tail, at_rest) in enumerate(layers):
        for c, part in enumerate(columns(at_qkv, 3)):
            qkv_ref[layer, :, c * TILE : (c + 1) * TILE] = part
        tail = columns(at_tail, 1)[0]
        tails.append(tail)
        qkv_ref[layer, :, MAXLAG:] = tail[:, :48]
        for c, part in enumerate(columns(at_rest, 3)):
            down_ref[layer, :, c * TILE : (c + 1) * TILE] = part
        for c, part in enumerate(columns(at_rest + 27, 6)):
            gate_up_ref[layer, :, c * TILE : (c + 1) * TILE] = part
        out_ref[layer, :, :TILE] = columns(at_rest + 81, 1)[0]
        out_ref[layer, :, TILE:] = tail[:, 48:64]
    lag = jnp.where(iota((1, TILE), 1) < 64, pltpu.roll(tails[0], 64, 1), tails[1])
    lag_ref[...] = lag[:, :FEATS]
    pick = (iota((8, TILE), 1) == iota((8, TILE), 0) + 96).astype(bf16)
    rest = nt(pick, tails[1].astype(bf16))
    gains_ref[0] = rest[0:2]
    gains_ref[1] = rest[2:4]
    scale_ref[...] = ((rest[4:5] + rest[5:6]) / rest[6:7])[:, :DATASETS]


def weights_kernel(
    traffic, lag_ref, w_lag_ref, w_qkv_ref, w_out_ref, w_gate_up_ref, cot_ref,
    dense_ref, qkv0_ref, out0_ref, gate_up0_ref, qkv1_ref, out1_ref, gate_up1_ref, chosen_ref, low_cot_ref,
):
    traffic.ready()
    rows = iota((FEATS, 1), 0)
    diagonal = iota((FEATS, LAGS), 0) == iota((FEATS, LAGS), 1)
    offsets = jnp.sum(jnp.where(diagonal, lag_ref[...].astype(f32), 0.0), axis=1, keepdims=True)
    offsets = jnp.where(rows < LAGS, offsets - 1.0, (rows - LAGS + MAXLAG + 1).astype(f32))
    chosen = (iota((FEATS, LAGCOLS), 1).astype(f32) == offsets).astype(bf16)
    chosen_ref[0:FEATS, :] = chosen
    chosen_ref[FEATS:, :] = jnp.zeros((96 - FEATS, LAGCOLS), bf16)
    dense_ref[...] = nn(w_lag_ref[...], chosen).astype(bf16)
    qkv0_ref[...] = turned(w_qkv_ref[0])
    out0_ref[...] = turned(w_out_ref[0])
    gate_up0_ref[...] = turned(w_gate_up_ref[0])
    qkv1_ref[...] = turned(w_qkv_ref[1])
    out1_ref[...] = turned(w_out_ref[1])
    gate_up1_ref[...] = turned(w_gate_up_ref[1])
    low_cot_ref[...] = cot_ref[...].astype(bf16)


def first_values_kernel(traffic, len_ref, scale_ref, raw_ref, hours_ref, out_ref):
    traffic.ready()
    places = lax.axis_index("tm") * TILE + iota((1, TILE), 1)
    own = doc_scale_at(places, len_ref, scale_ref)
    angle = hours_ref[...].astype(f32) * (2.0 * math.pi / 24.0)
    rows = [raw_ref[...] / own, jnp.sin(angle), jnp.cos(angle), jnp.log(own), jnp.zeros((4, TILE), f32)]
    out_ref[...] = jnp.broadcast_to(jnp.concatenate(rows, axis=0)[None], out_ref.shape)


def shape(*dims, dtype=f32):
    return jax.ShapeDtypeStruct(dims, dtype)


class Traffic:
    def __init__(self, loads, stores):
        self.loads, self.stores, self.waited, self.sent = loads, stores, 0, set()
        for copy in loads:
            copy.start()

    def ready(self, count=None):
        count = len(self.loads) if count is None else count
        for copy in self.loads[self.waited : count]:
            copy.wait()
        self.waited = max(self.waited, count)

    def send(self, *refs):
        for ref, copy in self.stores:
            if any(ref is r for r in refs):
                copy.start()
                self.sent.add(id(copy))

    def finish(self):
        self.ready()
        for _, copy in self.stores:
            if id(copy) not in self.sent:
                copy.start()
        for _, copy in self.stores:
            copy.wait()


def call(kernel, operands, outs, scratch=(), tables=(), weights=(), cost=None):
    several = isinstance(outs, list)
    outs = outs if several else [outs]
    layers = [None] * len(tables) + [x[1] if isinstance(x, tuple) else None for x in weights]
    fetched = (*tables, *(x[0] if isinstance(x, tuple) else x for x in weights))
    shapes = [x.shape if layer is None else x.shape[1:] for x, layer in zip(fetched, layers)]
    buffers = [(pltpu.SMEM if n < len(tables) else pltpu.VMEM)(shapes[n], x.dtype) for n, x in enumerate(fetched)]
    is_far = [not isinstance(out, jax.ShapeDtypeStruct) for out in outs]
    buffers += [pltpu.VMEM(out.shape, out.dtype) for out, far in zip(outs, is_far) if far]
    count, extra, copies = len(operands), len(buffers), len(buffers)

    def wrapped(*refs):
        refs = list(refs)
        ins, sources = refs[:count], refs[count : count + len(fetched)]
        results = refs[count + len(fetched) : count + len(fetched) + len(outs)]
        rest = refs[count + len(fetched) + len(outs) :]
        if not copies:
            kernel(*ins, *results, *rest)
            return
        own, held, sems = rest[: len(scratch)], rest[len(scratch) : -1], rest[-1]
        sources = [a if layer is None else a.at[layer] for a, layer in zip(sources, layers)]
        loads = [pltpu.make_async_copy(a, b, sems.at[n]) for n, (a, b) in enumerate(zip(sources, held))]
        stores, at = [], len(fetched)
        for n, far in enumerate(is_far):
            if far:
                stores.append((held[at], pltpu.make_async_copy(held[at], results[n], sems.at[at])))
                results[n] = held[at]
                at += 1
        traffic = Traffic(loads, stores)
        kernel(traffic, *ins, *held[: len(fetched)], *results, *own)
        traffic.finish()

    vmem, hbm = pl.BlockSpec(memory_space=pltpu.VMEM), pl.BlockSpec(memory_space=pltpu.HBM)
    results = pl.pallas_call(
        wrapped,
        out_shape=outs,
        in_specs=[vmem] * count + [hbm] * len(fetched),
        out_specs=[hbm if far else vmem for far in is_far],
        scratch_shapes=[*scratch, *buffers, pltpu.SemaphoreType.DMA((copies,))] if copies else list(scratch),
        compiler_params=pltpu.CompilerParams(vmem_limit_bytes=VMEM),
        cost_estimate=cost and pl.CostEstimate(flops=cost * 10**9, bytes_accessed=10**6, transcendentals=0),
    )(*operands, *(pltpu.with_memory_space_constraint(x, pltpu.HBM) for x in fetched))
    return results if several else results[0]


def pair_permute(x, bit):
    return lax.ppermute(x, "tm", [(i, i ^ bit) for i in range(32)])


def gather(copies, beside):
    groups = [[2 * chip for chip in range(16)], [31 - 2 * chip for chip in range(16)]]
    own = lax.all_to_all(copies, "tm", 0, 0, axis_index_groups=groups)
    own, beside = lax.optimization_barrier((own, beside))
    return own, pair_permute(own, 1), beside


def swap(block):
    return lax.ppermute(block, "tm", [(n, n if n % 2 == 0 else 32 - n) for n in range(32)])


def tile_halves(own, other):
    lane = iota((1, TILE), 1) < HALF
    return jnp.where(lane == (lax.axis_index("tm") < 16), own, other)


def rope_table():
    freqs = 10000.0 ** (-np.arange(8, dtype=np.float64) / 8)
    angle = np.arange(LEN, dtype=np.float64)[None, :] * freqs[:, None]
    return np.concatenate([np.cos(angle), np.sin(angle)], axis=0).astype(np.float32)


def body(
    raw_values, hours, doc_lengths, doc_scale, dataset_ids, lag_offsets, w_lag, w_qkv, w_out, w_gate_up, w_down, gains, cotangent
):
    lengths, scales, ids = doc_lengths.reshape(DOCS), doc_scale.reshape(DOCS), dataset_ids.reshape(DOCS)
    def low(*dims):
        return shape(*dims, dtype=bf16)

    def far(*dims, dtype=f32):
        return pltpu.HBM(dims, dtype)

    def far_low(*dims):
        return far(*dims, dtype=bf16)

    w_lag, w_down, lags = w_lag.T, w_down.transpose(0, 2, 1), lag_offsets.reshape(1, LAGS)
    rope = jnp.asarray(rope_table())
    values = lax.all_to_all(call(first_values_kernel, (), shape(32, 8, TILE), tables=(lengths, scales), weights=(raw_values, hours)), "tm", 0, 0)
    turned_shapes = [far_low(3 * D, D), far_low(D, D), far_low(2 * FF, D)]
    w_dense, *turned_weights, chosen, low_cot = call(
        weights_kernel, (), [far_low(D, LAGCOLS), *turned_shapes, *turned_shapes, far_low(96, LAGCOLS), far_low(D, TILE)],
        weights=(lags, w_lag, w_qkv, w_out, w_gate_up, cotangent[0].T), cost=3,
    )
    turned0, turned1 = turned_weights[:3], turned_weights[3:]
    values, w_dense = lax.optimization_barrier((values, w_dense))
    all_d = far_low(BLOCKS, D, BLOCK)
    mine, mine_low, ff_low, column_shape = far(D, TILE), far_low(D, TILE), far_low(FF, TILE), far(D, 1)
    payload_shapes = [far_low(16, AUG, TILE), far_low(AUG, TILE)]
    low_grads = [mine_low, far_low(2 * FF, TILE), mine_low, ff_low, mine_low]
    bd, wide_bd = pltpu.VMEM((2, ROWS, AUG), bf16), pltpu.VMEM((2, ROWS, WIDE), bf16)
    acc, acc_d = pltpu.VMEM((2, ROWS, AUG), f32), pltpu.VMEM((2, ROWS, D), f32)
    top = pltpu.VMEM((2, ROWS, 1), f32)
    back_scratch = [pltpu.VMEM((BLOCKS, AUG, BLOCK), bf16), wide_bd, bd, acc_d, acc]

    (copies, next1, resid1, keys0, values0, normal_all0, feats, resid0, normal_a0, q0, att0, stat0, mid0, gate_up0, own_rope) = call(
        first_kernel,
        (values,),
        [far_low(16, D, TILE), mine_low, mine, all_d, all_d, all_d, far_low(96, TILE), mine, mine_low, far_low(TILE, D), mine_low,
         far_low(STAT, TILE), mine, far(2 * FF, TILE), far(16, TILE)],
        [pltpu.VMEM((8 + TILES, TILE), f32), pltpu.VMEM((TILE, MAXLAG + LEN), bf16),
         pltpu.VMEM((LAGCOLS, TILE), bf16), wide_bd, top, acc],
        tables=(lengths,), weights=(w_dense, gains, turned0[0], rope, chosen, *turned0[1:], (w_down, 0)),
    )

    own, other, cot = gather(copies, swap(low_cot))
    copies, payload, act, keys1, values1, normal_all1, q1, grad, att1, d_gain_b1, *low1 = call(
        second_kernel,
        (own, other, cot, pair_permute(cot, 1)),
        [*payload_shapes, mine, all_d, all_d, all_d, far_low(TILE, D), mine, mine_low, column_shape, *low_grads],
        [wide_bd, top, acc],
        tables=(lengths,),
        weights=(turned1[0], rope, next1, own_rope, resid1, *turned1[1:], (w_out, 1), (w_gate_up, 1), (w_down, 1), gains),
    )

    rows_low = far_low(TILE, D)
    side_shapes = [mine, all_d, rows_low, rows_low]
    d_out, d_gate_up, d_branch, hidden, normal_b = low1
    pack, tail, dq, qall, k_rows, v_rows = call(
        second_window_kernel, (), [far_low(90, 16, TILE), mine, *side_shapes], [wide_bd, bd, acc_d],
        tables=(lengths,),
        weights=(hidden, d_out, normal_b, d_gate_up, att1, d_branch, d_gain_b1, payload, q1, own_rope, rope, keys1, values1, normal_all1,
                 turned1[0]), cost=8,
    )
    own, other, dq = gather(copies, dq)
    copies, payload, grad, d_mixed, d_gain_a1, d_gain_b0, *low0 = call(
        third_kernel,
        (own, other),
        [*payload_shapes, mine, far_low(3 * D, TILE), column_shape, column_shape, *low_grads],
        back_scratch,
        tables=(lengths,),
        weights=(qall, k_rows, v_rows, dq, grad, resid1, att0, stat0, mid0, gate_up0, own_rope, (w_qkv, 1), (w_out, 0), (w_gate_up, 0),
                 (w_down, 0), gains),
    )
    d_out, d_gate_up, d_branch, hidden, normal_b = low0
    early, early_out, rest, tail0, tail1, dq, qall, k_rows, v_rows = call(
        third_window_kernel, (),
        [far_low(EARLY, 16, TILE), far_low(EARLY, 16, TILE), far_low(1, 16, TILE), mine, mine, *side_shapes], [wide_bd, bd, acc_d],
        tables=(lengths,),
        weights=(pack, tail, next1, d_mixed, d_gain_a1, hidden, d_out, normal_b, d_gate_up, att0, d_branch, d_gain_b0, payload, q0,
                 own_rope, rope, keys0, values0, normal_all0, turned0[0]), cost=8,
    )
    own, other, (dq, early_out) = gather(copies, (dq, early_out))
    early_in = pair_permute(early_out, 1)
    late, late_out = call(
        last_kernel,
        (own, other),
        [low(LATE, 16, TILE)] * 2,
        [*back_scratch, pltpu.VMEM((2, 24, TILE), f32)],
        tables=(lengths, scales, ids),
        weights=(qall, k_rows, v_rows, dq, grad, resid0, normal_a0, tail0, tail1, rest, w_dense, feats, own_rope, (w_qkv, 0), gains),
    )
    packed = call(pair_sum_kernel, (early, early_in, late, pair_permute(late_out, 1)), low(64, 40, TILE))
    same_core = [[2 * chip for chip in range(64)], [127 - 2 * chip for chip in range(64)]]
    parts = lax.all_to_all(packed, ("series", "tm"), 0, 0, axis_index_groups=same_core)
    share, raw_grad = call(sum_kernel, (parts,), [low(64, 32, TILE), shape(1, TILE)])
    share, act = lax.optimization_barrier((share, act))
    own = lax.all_to_all(share, ("series", "tm"), 0, 0, axis_index_groups=same_core)
    own, act = lax.optimization_barrier((own, swap(tile_halves(act, pair_permute(act, 1)))))
    act, g_lag, g_qkv, g_out, g_gate_up, g_down, g_gains, scale = call(
        unpack_kernel,
        (own, pair_permute(own, 1), act),
        [shape(D, TILE), shape(D, FEATS), shape(LAYERS, D, 3 * D), shape(LAYERS, D, D), shape(LAYERS, D, 2 * FF), shape(LAYERS, D, FF),
         shape(LAYERS, 2, D), shape(1, DATASETS)],
    )
    return (
        act.T[None], raw_grad, scale.reshape(DATASETS), g_lag.T, g_qkv, g_out, g_gate_up, g_down.transpose(0, 2, 1), g_gains,
    )


def solution(mesh):
    placed = (
        P("series", "tm"),
        P("series", "tm"),
        P("series", None),
        P("series", None),
        P("series", None, None),
        P(),
        P(),
        P(),
        P(),
        P(),
        P(),
        P(),
        P("series", "tm", None),
    )
    return jax.shard_map(
        body,
        mesh=mesh,
        in_specs=placed,
        out_specs=(P("series", "tm", None), P("series", "tm"), P(), P(), P(), P(), P(), P(), P()),
        check_vma=False,
    )
```

profile of v0, /device:TPU:1, one launch (start us, length us, event | category | flops | bytes accessed | tf_op | source)
XLA Modules:
  0.0 160.7 jit_solution(3392925830969962561)
XLA Ops:
  0.6 1.4 shard_map.205
  2.1 9.6 %all-to-all-start = ((f32[32,8,128]{2,1,0:T(8,128)}), f32[32,8,128]{2,1,0:T(8,128)S(1)}, u32[]{:S(2)}, u32[]{:S(2)}) async-start(f32[32,8,128]{2,1,0:T(8,128)} %shard_map.205), calls=%async_computation | async-start | bytes 262144 | tf_op jit(solution)/shard_map/all_to_all | solution.py:950
  11.7 2.9 %shard_map.206 = (bf16[144,400]{1,0:T(8,128)(2,1)}, bf16[432,144]{1,0:T(8,128)(2,1)}, bf16[144,144]{1,0:T(8,128)(2,1)}, bf16[768,144]{1,0:T(8,128)(2,1)}, bf16[4...) custom-call(s32[1,84]{1,0:T(1,128)} %bitcast.33, ...), custom_call_target="tpu_custom_call" | custom-call | flops 3000000000 | bytes 1000000 | tf_op jit(solution)/shard_map/pallas_call | solution.py:897
  14.6 4.8 %all-to-all-done.refs_0_ = f32[32,8,128]{2,1,0:T(8,128)S(1)} async-done(((f32[32,8,128]{2,1,0:T(8,128)}), f32[32,8,128]{2,1,0:T(8,128)S(1)}, u32[]{:S(2)}, u32[]{:S(2)}) %all-to-all-start) | async-done | bytes 131104 | tf_op jit(solution)/shard_map/all_to_all | solution.py:950
  19.3 10.7 %shard_map.207 = (bf16[16,144,128]{2,1,0:T(8,128)(2,1)}, bf16[144,128]{1,0:T(8,128)(2,1)}, f32[144,128]{1,0:T(8,128)}, bf16[8,144,512]{2,1,0:T(8,128)(2,1)}, bf1...) custom-call(f32[32,8,128]{2,1,0:T(8,128)S(1)} %all-to-all-done.refs_, ...), custom_call_target="tpu_custom_call" | custom-call | tf_op jit(solution)/shard_map/pallas_call | solution.py:897
  30.1 6.2 %all-to-all-start.1 = ((bf16[16,144,128]{2,1,0:T(8,128)(2,1)}), bf16[16,144,128]{2,1,0:T(8,128)(2,1)S(1)}, u32[]{:S(2)}, u32[]{:S(2)}) async-start(bf16[16,144,128]{2,1,0:T(8,128)(2,1)} %get-tuple-element.106), calls=%async_computation.1 | async-start | bytes 1179648 | tf_op jit(solution)/shard_map/all_to_all | solution.py:915
  36.3 2.0 %collective-permute-start = (bf16[144,128]{1,0:T(8,128)(2,1)S(1)}, bf16[144,128]{1,0:T(8,128)(2,1)S(1)}, u32[]{:S(2)}, u32[]{:S(2)}) collective-permute-start(bf16[144,128]{1,0:T(8,128)(2,1)S(1)} %copy-done.2), channel_id=1, source_target_pairs={{0,0},{1,31},{2,2},{3,29},{4,4},{5,27},{6,6},{7,25},{8,8},{9,23},{... | collective-permute-start | bytes 110600 | tf_op jit(solution)/shard_map/ppermute | solution.py:921
  38.3 6.0 %collective-permute-done.refs_2_ = bf16[144,128]{1,0:T(8,128)(2,1)S(1)} collective-permute-done((bf16[144,128]{1,0:T(8,128)(2,1)S(1)}, bf16[144,128]{1,0:T(8,128)(2,1)S(1)}, u32[]{:S(2)}, u32[]{:S(2)}) %collective-permute-start) | collective-permute-done | bytes 36896 | tf_op jit(solution)/shard_map/ppermute | solution.py:921
  44.4 0.8 all-to-all-done.1.refs_0_
  45.2 0.5 collective-permute-start.1
  45.7 1.7 %collective-permute-done.2.refs_3_ = bf16[144,128]{1,0:T(8,128)(2,1)S(1)} collective-permute-done((bf16[144,128]{1,0:T(8,128)(2,1)S(1)}, bf16[144,128]{1,0:T(8,128)(2,1)S(1)}, u32[]{:S(2)}, u32[]{:S(2)}) %collective-permute-start.2) | collective-permute-done | bytes 36896 | tf_op jit(solution)/shard_map/ppermute | solution.py:910
  47.4 9.2 %shard_map.208 = (bf16[16,176,128]{2,1,0:T(8,128)(2,1)}, bf16[176,128]{1,0:T(8,128)(2,1)}, f32[144,128]{1,0:T(8,128)}, bf16[8,144,512]{2,1,0:T(8,128)(2,1)}, bf1...) custom-call(bf16[16,144,128]{2,1,0:T(8,128)(2,1)S(1)} %all-to-all-do, ...), custom_call_target="tpu_custom_call" | custom-call | tf_op jit(solution)/shard_map/pallas_call | solution.py:897
  56.6 6.7 %all-to-all-start.2 = ((bf16[16,176,128]{2,1,0:T(8,128)(2,1)}), bf16[16,176,128]{2,1,0:T(8,128)(2,1)S(1)}, u32[]{:S(2)}, u32[]{:S(2)}) async-start(bf16[16,176,128]{2,1,0:T(8,128)(2,1)} %get-tuple-element.130), calls=%async_computation.2 | async-start | bytes 1441792 | tf_op jit(solution)/shard_map/all_to_all | solution.py:915
  63.3 10.7 %shard_map.209 = (bf16[90,16,128]{2,1,0:T(8,128)(2,1)}, f32[144,128]{1,0:T(8,128)}, f32[144,128]{1,0:T(8,128)}, bf16[8,144,512]{2,1,0:T(8,128)(2,1)}, bf16[128,1...) custom-call(s32[7]{0:T(128)} %bitcast.21, bf16[384,128]{1,0:T(8,128)(2,1)} %get-tuple-element.116.refs_1_, ...), custom_call_target="tpu_custom_call" | custom-call | flops 8000000000 | bytes 1000000 | tf_op jit(solution)/shard_map/pallas_call | solution.py:897
  74.2 2.2 %collective-permute-done.3.refs_1_ = bf16[16,176,128]{2,1,0:T(8,128)(2,1)S(1)} collective-permute-done((bf16[16,176,128]{2,1,0:T(8,128)(2,1)S(1)}, bf16[16,176,128]{2,1,0:T(8,128)(2,1)S(1)}, u32[]{:S(2)}, u32[]{:S(2)}) %collective-permute-start.3) | collective-permute-done | bytes 720928 | tf_op jit(solution)/shard_map/ppermute | solution.py:910
  76.3 9.8 %shard_map.210 = (bf16[16,176,128]{2,1,0:T(8,128)(2,1)}, bf16[176,128]{1,0:T(8,128)(2,1)}, f32[144,128]{1,0:T(8,128)}, bf16[432,128]{1,0:T(8,128)(2,1)}, f32[144...) custom-call(bf16[16,176,128]{2,1,0:T(8,128)(2,1)S(1)} %all-to-all-do, ...), custom_call_target="tpu_custom_call" | custom-call | tf_op jit(solution)/shard_map/pallas_call | solution.py:897
  86.1 6.7 %all-to-all-start.3 = ((bf16[16,176,128]{2,1,0:T(8,128)(2,1)}), bf16[16,176,128]{2,1,0:T(8,128)(2,1)S(1)}, u32[]{:S(2)}, u32[]{:S(2)}) async-start(bf16[16,176,128]{2,1,0:T(8,128)(2,1)} %get-tuple-element.156), calls=%async_computation.3 | async-start | bytes 1441792 | tf_op jit(solution)/shard_map/all_to_all | solution.py:915
  92.8 10.8 %shard_map.211 = (bf16[103,16,128]{2,1,0:T(8,128)(2,1)}, bf16[103,16,128]{2,1,0:T(8,128)(2,1)}, bf16[1,16,128]{2,1,0:T(8,128)(2,1)}, f32[144,128]{1,0:T(8,128)},...) custom-call(s32[7]{0:T(128)} %bitcast.23, ...), custom_call_target="tpu_custom_call" | custom-call | flops 8000000000 | bytes 1000000 | tf_op jit(solution)/shard_map/pallas_call | solution.py:897
  103.8 0.5 collective-permute-start.4
  104.2 1.8 %collective-permute-done.5.refs_1_ = bf16[16,176,128]{2,1,0:T(8,128)(2,1)S(1)} collective-permute-done((bf16[16,176,128]{2,1,0:T(8,128)(2,1)S(1)}, bf16[16,176,128]{2,1,0:T(8,128)(2,1)S(1)}, u32[]{:S(2)}, u32[]{:S(2)}) %collective-permute-start.5) | collective-permute-done | bytes 720928 | tf_op jit(solution)/shard_map/ppermute | solution.py:910
  106.0 8.9 %shard_map.212 = (bf16[24,16,128]{2,1,0:T(8,128)(2,1)S(1)}, bf16[24,16,128]{2,1,0:T(8,128)(2,1)S(1)}) custom-call(bf16[16,176,128]{2,1,0:T(8,128)(2,1)S(1)} %all-to-all-done.3.refs_0_, bf16[16,176,128]{2,1,0:T(8,128)(2,1)S(1)} %collective-permute-done.5.refs_1_, s32[7]{0:T(128)} %bitcast.24, f32[7]{0:T(128)} %bitcast.26, s32[7]{0:T(128)} %bitcast.27, ...), custom_call_target="tpu_custom_call" | custom-call | tf_op jit(solution)/shard_map/pallas_call | solution.py:897
  114.9 0.2 collective-permute-start.6
  115.1 1.2 collective-permute-done.6.refs_3_
  116.3 0.1 shard_map.213
  116.4 19.4 %all_to_all.30.refs_0_ = bf16[64,40,128]{2,1,0:T(8,128)(2,1)S(1)} all-to-all(bf16[64,40,128]{2,1,0:T(8,128)(2,1)S(1)} %shard_map.213), channel_id=1, replica_groups={{0,2,4,6,8,10,12,14,16,18,20,22,24,26,28,30,32,34,36,38,40,42,44,46,48,..., dimensions={0} | all-to-all | bytes 1310720 | tf_op jit(solution)/shard_map/all_to_all | solution.py:1026
  135.9 0.9 shard_map.214
  136.8 10.4 %all-to-all-start.5 = ((bf16[64,32,128]{2,1,0:T(8,128)(2,1)}), bf16[64,32,128]{2,1,0:T(8,128)(2,1)S(1)}, u32[]{:S(2)}, u32[]{:S(2)}) async-start(bf16[64,32,128]{2,1,0:T(8,128)(2,1)} %get-tuple-element.176), calls=%async_computation.5 | async-start | bytes 1048576 | tf_op jit(solution)/shard_map/all_to_all | solution.py:1029
  147.4 1.2 collective-permute-done.7
  148.6 4.5 %collective-permute-start.8 = (f32[144,128]{1,0:T(8,128)S(1)}, f32[144,128]{1,0:T(8,128)S(1)}, u32[]{:S(2)}, u32[]{:S(2)}) collective-permute-start(f32[144,128]{1,0:T(8,128)S(1)} %broadcast_select_fusion), channel_id=1, source_target_pairs={{0,0},{1,31},{2,2},{3,29},{4,4},{5,27},{6,6},{7,25},{8,8},{9,23},{... | collective-permute-start | bytes 221192 | tf_op jit(solution)/shard_map/ppermute | solution.py:921
  153.1 4.2 %collective-permute-done.8.refs_2_ = f32[144,128]{1,0:T(8,128)S(1)} collective-permute-done((f32[144,128]{1,0:T(8,128)S(1)}, f32[144,128]{1,0:T(8,128)S(1)}, u32[]{:S(2)}, u32[]{:S(2)}) %collective-permute-start.8) | collective-permute-done | bytes 73760 | tf_op jit(solution)/shard_map/ppermute | solution.py:921
  157.4 1.9 %collective-permute-done.9.refs_1_ = bf16[64,32,128]{2,1,0:T(8,128)(2,1)S(1)} collective-permute-done((bf16[64,32,128]{2,1,0:T(8,128)(2,1)S(1)}, bf16[64,32,128]{2,1,0:T(8,128)(2,1)S(1)}, u32[]{:S(2)}, u32[]{:S(2)}) %collective-permute-start.9) | collective-permute-done | bytes 524320 | tf_op jit(solution)/shard_map/ppermute | solution.py:910
  159.2 1.5 shard_map.215
  (18 shorter events, 0.4 us)
Async XLA Ops:
  2.1 17.2 %all-to-all-start = ((f32[32,8,128]{2,1,0:T(8,128)}), f32[32,8,128]{2,1,0:T(8,128)S(1)}, u32[]{:S(2)}, u32[]{:S(2)}) async-start(f32[32,8,128]{2,1,0:T(8,128)} %shard_map.205), calls=%async_computation | async-start | bytes 262144 | tf_op jit(solution)/shard_map/all_to_all | solution.py:950
  19.3 17.0 %copy-start.2 = (bf16[144,128]{1,0:T(8,128)(2,1)S(1)}, bf16[144,128]{1,0:T(8,128)(2,1)}, u32[]{:S(2)}) copy-start(bf16[144,128]{1,0:T(8,128)(2,1)} %get-tuple-element.107) | copy-start | bytes 110596
  30.1 15.1 %all-to-all-start.1 = ((bf16[16,144,128]{2,1,0:T(8,128)(2,1)}), bf16[16,144,128]{2,1,0:T(8,128)(2,1)S(1)}, u32[]{:S(2)}, u32[]{:S(2)}) async-start(bf16[16,144,128]{2,1,0:T(8,128)(2,1)} %get-tuple-element.106), calls=%async_computation.1 | async-start | bytes 1179648 | tf_op jit(solution)/shard_map/all_to_all | solution.py:915
  36.3 8.1 %collective-permute-start = (bf16[144,128]{1,0:T(8,128)(2,1)S(1)}, bf16[144,128]{1,0:T(8,128)(2,1)S(1)}, u32[]{:S(2)}, u32[]{:S(2)}) collective-permute-start(bf16[144,128]{1,0:T(8,128)(2,1)S(1)} %copy-done.2), channel_id=1, source_target_pairs={{0,0},{1,31},{2,2},{3,29},{4,4},{5,27},{6,6},{7,25},{8,8},{9,23},{... | collective-permute-start | bytes 110600 | tf_op jit(solution)/shard_map/ppermute | solution.py:921
  45.2 2.2 %collective-permute-start.1 = (bf16[16,144,128]{2,1,0:T(8,128)(2,1)S(1)}, bf16[16,144,128]{2,1,0:T(8,128)(2,1)S(1)}, u32[]{:S(2)}, u32[]{:S(2)}) collective-permute-start(bf16[16,144,128]{2,1,0:T(8,128)(2,1)S(1)} %all-to-all-done.1.refs_0_), channel_id=1, source_target_pairs={{0,1},{1,0},{2,3},{3,2},{4,5},{5,4},{6,7},{7,6},{8,9},{9,8},{10,11... | collective-permute-start | bytes 1769480 | tf_op jit(solution)/shard_map/ppermute | solution.py:910
  45.7 1.7 %collective-permute-start.2 = (bf16[144,128]{1,0:T(8,128)(2,1)S(1)}, bf16[144,128]{1,0:T(8,128)(2,1)S(1)}, u32[]{:S(2)}, u32[]{:S(2)}) collective-permute-start(bf16[144,128]{1,0:T(8,128)(2,1)S(1)} %collective-permute-done.refs_2_), channel_id=1, source_target_pairs={{0,1},{1,0},{2,3},{3,2},{4,5},{5,4},{6,7},{7,6},{8,9},{9,8},{10,11... | collective-permute-start | bytes 110600 | tf_op jit(solution)/shard_map/ppermute | solution.py:910
  56.6 17.4 %all-to-all-start.2 = ((bf16[16,176,128]{2,1,0:T(8,128)(2,1)}), bf16[16,176,128]{2,1,0:T(8,128)(2,1)S(1)}, u32[]{:S(2)}, u32[]{:S(2)}) async-start(bf16[16,176,128]{2,1,0:T(8,128)(2,1)} %get-tuple-element.130), calls=%async_computation.2 | async-start | bytes 1441792 | tf_op jit(solution)/shard_map/all_to_all | solution.py:915
  74.1 2.3 %collective-permute-start.3 = (bf16[16,176,128]{2,1,0:T(8,128)(2,1)S(1)}, bf16[16,176,128]{2,1,0:T(8,128)(2,1)S(1)}, u32[]{:S(2)}, u32[]{:S(2)}) collective-permute-start(bf16[16,176,128]{2,1,0:T(8,128)(2,1)S(1)} %all-to-all-done.2.refs_0_), channel_id=1, source_target_pairs={{0,1},{1,0},{2,3},{3,2},{4,5},{5,4},{6,7},{7,6},{8,9},{9,8},{10,11... | collective-permute-start | bytes 2162696 | tf_op jit(solution)/shard_map/ppermute | solution.py:910
  86.1 17.5 %all-to-all-start.3 = ((bf16[16,176,128]{2,1,0:T(8,128)(2,1)}), bf16[16,176,128]{2,1,0:T(8,128)(2,1)S(1)}, u32[]{:S(2)}, u32[]{:S(2)}) async-start(bf16[16,176,128]{2,1,0:T(8,128)(2,1)} %get-tuple-element.156), calls=%async_computation.3 | async-start | bytes 1441792 | tf_op jit(solution)/shard_map/all_to_all | solution.py:915
  103.7 2.4 %collective-permute-start.5 = (bf16[16,176,128]{2,1,0:T(8,128)(2,1)S(1)}, bf16[16,176,128]{2,1,0:T(8,128)(2,1)S(1)}, u32[]{:S(2)}, u32[]{:S(2)}) collective-permute-start(bf16[16,176,128]{2,1,0:T(8,128)(2,1)S(1)} %all-to-all-done.3.refs_0_), channel_id=1, source_target_pairs={{0,1},{1,0},{2,3},{3,2},{4,5},{5,4},{6,7},{7,6},{8,9},{9,8},{10,11... | collective-permute-start | bytes 2162696 | tf_op jit(solution)/shard_map/ppermute | solution.py:910
  103.8 11.4 %collective-permute-start.4 = (bf16[103,16,128]{2,1,0:T(8,128)(2,1)}, bf16[103,16,128]{2,1,0:T(8,128)(2,1)S(1)}, u32[]{:S(2)}, u32[]{:S(2)}) collective-permute-start(bf16[103,16,128]{2,1,0:T(8,128)(2,1)} %get-tuple-element.159), channel_id=1, source_target_pairs={{0,1},{1,0},{2,3},{3,2},{4,5},{5,4},{6,7},{7,6},{8,9},{9,8},{10,11... | collective-permute-start | bytes 1265672 | tf_op jit(solution)/shard_map/ppermute | solution.py:910
  106.0 10.3 %copy-start = (bf16[103,16,128]{2,1,0:T(8,128)(2,1)S(1)}, bf16[103,16,128]{2,1,0:T(8,128)(2,1)}, u32[]{:S(2)}) copy-start(bf16[103,16,128]{2,1,0:T(8,128)(2,1)} %get-tuple-element.155.refs_0_) | copy-start | bytes 1265668
  114.9 1.4 collective-permute-start.6
  135.9 11.4 %copy-start.1 = (f32[144,128]{1,0:T(8,128)S(1)}, f32[144,128]{1,0:T(8,128)}, u32[]{:S(2)}) copy-start(f32[144,128]{1,0:T(8,128)} %get-tuple-element.177) | copy-start | bytes 221188
  136.8 20.5 %all-to-all-start.5 = ((bf16[64,32,128]{2,1,0:T(8,128)(2,1)}), bf16[64,32,128]{2,1,0:T(8,128)(2,1)S(1)}, u32[]{:S(2)}, u32[]{:S(2)}) async-start(bf16[64,32,128]{2,1,0:T(8,128)(2,1)} %get-tuple-element.176), calls=%async_computation.5 | async-start | bytes 1048576 | tf_op jit(solution)/shard_map/all_to_all | solution.py:1029
  147.3 1.3 collective-permute-start.7
  148.6 8.7 %collective-permute-start.8 = (f32[144,128]{1,0:T(8,128)S(1)}, f32[144,128]{1,0:T(8,128)S(1)}, u32[]{:S(2)}, u32[]{:S(2)}) collective-permute-start(f32[144,128]{1,0:T(8,128)S(1)} %broadcast_select_fusion), channel_id=1, source_target_pairs={{0,0},{1,31},{2,2},{3,29},{4,4},{5,27},{6,6},{7,25},{8,8},{9,23},{... | collective-permute-start | bytes 221192 | tf_op jit(solution)/shard_map/ppermute | solution.py:921
  157.3 1.9 %collective-permute-start.9 = (bf16[64,32,128]{2,1,0:T(8,128)(2,1)S(1)}, bf16[64,32,128]{2,1,0:T(8,128)(2,1)S(1)}, u32[]{:S(2)}, u32[]{:S(2)}) collective-permute-start(bf16[64,32,128]{2,1,0:T(8,128)(2,1)S(1)} %all-to-all-done.5.refs_0_), channel_id=1, source_target_pairs={{0,1},{1,0},{2,3},{3,2},{4,5},{5,4},{6,7},{7,6},{8,9},{9,8},{10,11... | collective-permute-start | bytes 1572872 | tf_op jit(solution)/shard_map/ppermute | solution.py:910
where the time goes:
time: 161 us
  Pallas kernels  67.1 us (42%)
  starting transfers between devices  47.7 us (30%)
  waiting for transfers between devices  25.7 us (16%)
  blocking collectives  19.4 us (12%)
    pallas_call x11, Pallas kernels, call(): pl.pallas_call(wrapped, out_shape=outs, in_specs=[vmem] * count + [hbm] *...  67.1 us
    all_to_all x3, starting transfers between devices, gather(): own = lax.all_to_all(copies, 'tm', 0, 0, axis_index_groups=groups)  19.6 us
    all_to_all x1, blocking collectives, body(): lax.all_to_all(packed, ('series', 'tm'), 0, 0, axis_index_groups=same_core)  19.4 us
    all_to_all x1, starting transfers between devices, body(): lax.all_to_all(share, ('series', 'tm'), 0, 0, axis_index_groups=same_core)  10.4 us
    ppermute x2, waiting for transfers between devices, swap(): lax.ppermute(block, 'tm', [(n, n if n % 2 == 0 else 32 - n) for n in rang...  10.2 us
    ppermute x8, waiting for transfers between devices, pair_permute(): return lax.ppermute(x, 'tm', [(i, i ^ bit) for i in range(32)])  9.87 us
    all_to_all x1, starting transfers between devices, body(): lax.all_to_all(call(first_values_kernel, (), shape(32, 8, TILE), tables=(...  9.61 us
    ppermute x2, starting transfers between devices, swap(): lax.ppermute(block, 'tm', [(n, n if n % 2 == 0 else 32 - n) for n in rang...  6.49 us
  transfers between devices with their start and end apart: 15, of which 10 were waited for; matrix products, arithmetic and copies ran while one was open for 0% of the time, Pallas kernels for 21%

commit v1 on v0

--- a/solution.py
+++ b/solution.py
@@ -38,7 +38,7 @@
 EARLY = 103
 LATE = 24
 WIDE = AUG + HALF
-SAFE = 40.0
+SAFE = 70.0
 VMEM = 28 * 2**20
 
 bf16 = jnp.bfloat16
@@ -209,7 +209,7 @@
     keys = rotate(mixed[:D], rope_ref[0:8, at], rope_ref[8:16, at])
     keys_ref[k] = keys.astype(bf16)
     values_ref[k] = mixed[D:].astype(bf16)
-    return head_sizes(keys)
+    return head_sizes(keys * keys)
 
 
 def query_of(normal, w_qkv, cosine, sine):
@@ -287,15 +287,16 @@
     return late.astype(jnp.int32), tile, tile // 4, slice(BLOCK // 2, BLOCK)
 
 
-def head_sizes(x):
-    return jnp.sum((x * x).reshape(HEADS, HEAD_DIM, x.shape[1]), axis=1)
+def head_sizes(squares):
+    return jnp.sum(squares.reshape(HEADS, HEAD_DIM, squares.shape[1]), axis=1)
 
 
 def attend(query, k_size, keys_ref, values_ref, len_ref, low, high, qbd, top_ref, acc_ref, q_rows_ref):
     q_rows = nt(eye(TILE, TILE, bf16), query)
     q_rows_ref[...] = q_rows.astype(bf16)
     spread(qbd, jnp.concatenate([q_rows, jnp.zeros((TILE, STAT), f32)], axis=1))
-    q_size = jnp.max(head_sizes(query.astype(f32)), axis=1, keepdims=True)
+    query = query.astype(f32)
+    q_size = jnp.max(head_sizes(query * query), axis=1, keepdims=True)
     k_size = jnp.max(k_size, axis=1, keepdims=True)
     acc_ref[...] = jnp.zeros(acc_ref.shape, f32)
     safe = jnp.max(q_size * k_size) <= SAFE * SAFE
@@ -308,7 +309,7 @@
             scores = scores_of(qbd[u], with_ones(keys_ref[block, :, at]), query_bias(u, tile, block, at, len_ref))
             acc_ref[u] = acc_ref[u] + nt(jnp.exp(scores).astype(bf16), with_ones(values_ref[block, :, at]))
 
-        run_steps(query_step, low, high, step)
+        run_steps(query_step, low, high, step, 8)
         step(*query_last(low, high))
 
     @pl.when(jnp.logical_not(safe))
@@ -333,18 +334,22 @@
         lax.fori_loop(0, STEPS * HEADS, step, 0)
 
     attended, stats = [], []
-    lane = iota((1, STAT), 1)
+    lane, col = iota((1, STAT), 1), iota((1, D), 1) // HEAD_DIM
     for u in range(2):
-        acc = acc_ref[u]
-        total = acc[:, D : D + 1]
-        attended.append(own_heads(acc[:, :D] / total))
-        parts = two_parts(-(top_ref[u] + jnp.log(total)))
-        stat = jnp.zeros((HALF, STAT), f32)
-        for j in range(2):
-            part = parts[j].astype(f32)
-            for h in range(HEADS):
-                stat = jnp.where(lane == 9 * j + h, part[h * HALF : (h + 1) * HALF], stat)
-        stats.append(stat)
+        acc, top = acc_ref[u], top_ref[u]
+        total, shift = jnp.ones((HALF, STAT), f32), jnp.zeros((HALF, STAT), f32)
+        for h in range(HEADS):
+            rows = slice(h * HALF, (h + 1) * HALF)
+            here = (lane == h) | (lane == HEADS + h)
+            total = jnp.where(here, acc[rows, D : D + 1], total)
+            shift = jnp.where(here, top[rows], shift)
+        hi, lo = two_parts(-(shift + jnp.log(total)))
+        stats.append(jnp.where(lane < HEADS, hi.astype(f32), jnp.where(lane < 2 * HEADS, lo.astype(f32), 0.0)))
+        own = jnp.zeros((HALF, D), f32)
+        for h in range(HEADS):
+            rows = slice(h * HALF, (h + 1) * HALF)
+            own = jnp.where(col == h, acc[rows, :D] / acc[rows, D : D + 1], own)
+        attended.append(own)
     att_rows = jnp.concatenate(attended, axis=0).astype(bf16)
     stat_rows = jnp.concatenate(stats, axis=0).astype(bf16)
     return nt(eye(D, D, bf16), att_rows).astype(bf16), nt(eye(STAT, STAT, bf16), stat_rows).astype(bf16)

time: 161 us -> 160 us (level)
  no operation moved by 1% of the time
where the time goes in v1:
time: 160 us; the launch traced here: 159 us
  Pallas kernels  65.6 us (41%)
  starting transfers between devices  47.7 us (30%)
  waiting for transfers between devices  25.6 us (16%)
  blocking collectives  19.7 us (12%)
    pallas_call x11, Pallas kernels, call(): pl.pallas_call(wrapped, out_shape=outs, in_specs=[vmem] * count + [hbm] *...  65.6 us
    all_to_all x1, blocking collectives, body(): lax.all_to_all(packed, ('series', 'tm'), 0, 0, axis_index_groups=same_core)  19.7 us
    all_to_all x3, starting transfers between devices, gather(): own = lax.all_to_all(copies, 'tm', 0, 0, axis_index_groups=groups)  19.7 us
    ppermute x2, waiting for transfers between devices, swap(): lax.ppermute(block, 'tm', [(n, n if n % 2 == 0 else 32 - n) for n in rang...  10.2 us
    all_to_all x1, starting transfers between devices, body(): lax.all_to_all(share, ('series', 'tm'), 0, 0, axis_index_groups=same_core)  10.1 us
    ppermute x8, waiting for transfers between devices, pair_permute(): return lax.ppermute(x, 'tm', [(i, i ^ bit) for i in range(32)])  9.76 us
    all_to_all x1, starting transfers between devices, body(): lax.all_to_all(call(first_values_kernel, (), shape(32, 8, TILE), tables=(...  9.61 us
    ppermute x2, starting transfers between devices, swap(): lax.ppermute(block, 'tm', [(n, n if n % 2 == 0 else 32 - n) for n in rang...  6.56 us
  transfers between devices with their start and end apart: 15, of which 10 were waited for; matrix products, arithmetic and copies ran while one was open for 0% of the time, Pallas kernels for 21%

profile of v1, /device:TPU:1, one launch (start us, length us, event | category | flops | bytes accessed | tf_op | source)
XLA Modules:
  0.0 159.4 jit_solution(15289876128991033663)
XLA Ops:
  0.6 1.4 shard_map.205
  2.1 9.6 %all-to-all-start = ((f32[32,8,128]{2,1,0:T(8,128)}), f32[32,8,128]{2,1,0:T(8,128)S(1)}, u32[]{:S(2)}, u32[]{:S(2)}) async-start(f32[32,8,128]{2,1,0:T(8,128)} %shard_map.205), calls=%async_computation | async-start | bytes 262144 | tf_op jit(solution)/shard_map/all_to_all | solution.py:955
  11.7 2.9 %shard_map.206 = (bf16[144,400]{1,0:T(8,128)(2,1)}, bf16[432,144]{1,0:T(8,128)(2,1)}, bf16[144,144]{1,0:T(8,128)(2,1)}, bf16[768,144]{1,0:T(8,128)(2,1)}, bf16[4...) custom-call(s32[1,84]{1,0:T(1,128)} %bitcast.33, ...), custom_call_target="tpu_custom_call" | custom-call | flops 3000000000 | bytes 1000000 | tf_op jit(solution)/shard_map/pallas_call | solution.py:902
  14.6 4.8 %all-to-all-done.refs_0_ = f32[32,8,128]{2,1,0:T(8,128)S(1)} async-done(((f32[32,8,128]{2,1,0:T(8,128)}), f32[32,8,128]{2,1,0:T(8,128)S(1)}, u32[]{:S(2)}, u32[]{:S(2)}) %all-to-all-start) | async-done | bytes 131104 | tf_op jit(solution)/shard_map/all_to_all | solution.py:955
  19.3 10.1 %shard_map.207 = (bf16[16,144,128]{2,1,0:T(8,128)(2,1)}, bf16[144,128]{1,0:T(8,128)(2,1)}, f32[144,128]{1,0:T(8,128)}, bf16[8,144,512]{2,1,0:T(8,128)(2,1)}, bf1...) custom-call(f32[32,8,128]{2,1,0:T(8,128)S(1)} %all-to-all-done.refs_, ...), custom_call_target="tpu_custom_call" | custom-call | tf_op jit(solution)/shard_map/pallas_call | solution.py:902
  29.4 6.3 %all-to-all-start.1 = ((bf16[16,144,128]{2,1,0:T(8,128)(2,1)}), bf16[16,144,128]{2,1,0:T(8,128)(2,1)S(1)}, u32[]{:S(2)}, u32[]{:S(2)}) async-start(bf16[16,144,128]{2,1,0:T(8,128)(2,1)} %get-tuple-element.106), calls=%async_computation.1 | async-start | bytes 1179648 | tf_op jit(solution)/shard_map/all_to_all | solution.py:920
  35.7 2.0 %collective-permute-start = (bf16[144,128]{1,0:T(8,128)(2,1)S(1)}, bf16[144,128]{1,0:T(8,128)(2,1)S(1)}, u32[]{:S(2)}, u32[]{:S(2)}) collective-permute-start(bf16[144,128]{1,0:T(8,128)(2,1)S(1)} %copy-done.2), channel_id=1, source_target_pairs={{0,0},{1,31},{2,2},{3,29},{4,4},{5,27},{6,6},{7,25},{8,8},{9,23},{... | collective-permute-start | bytes 110600 | tf_op jit(solution)/shard_map/ppermute | solution.py:926
  37.7 6.0 %collective-permute-done.refs_2_ = bf16[144,128]{1,0:T(8,128)(2,1)S(1)} collective-permute-done((bf16[144,128]{1,0:T(8,128)(2,1)S(1)}, bf16[144,128]{1,0:T(8,128)(2,1)S(1)}, u32[]{:S(2)}, u32[]{:S(2)}) %collective-permute-start) | collective-permute-done | bytes 36896 | tf_op jit(solution)/shard_map/ppermute | solution.py:926
  43.7 0.8 all-to-all-done.1.refs_0_
  44.6 0.5 collective-permute-start.1
  45.1 1.7 %collective-permute-done.2.refs_3_ = bf16[144,128]{1,0:T(8,128)(2,1)S(1)} collective-permute-done((bf16[144,128]{1,0:T(8,128)(2,1)S(1)}, bf16[144,128]{1,0:T(8,128)(2,1)S(1)}, u32[]{:S(2)}, u32[]{:S(2)}) %collective-permute-start.2) | collective-permute-done | bytes 36896 | tf_op jit(solution)/shard_map/ppermute | solution.py:915
  46.7 8.5 %shard_map.208 = (bf16[16,176,128]{2,1,0:T(8,128)(2,1)}, bf16[176,128]{1,0:T(8,128)(2,1)}, f32[144,128]{1,0:T(8,128)}, bf16[8,144,512]{2,1,0:T(8,128)(2,1)}, bf1...) custom-call(bf16[16,144,128]{2,1,0:T(8,128)(2,1)S(1)} %all-to-all-do, ...), custom_call_target="tpu_custom_call" | custom-call | tf_op jit(solution)/shard_map/pallas_call | solution.py:902
  55.2 6.7 %all-to-all-start.2 = ((bf16[16,176,128]{2,1,0:T(8,128)(2,1)}), bf16[16,176,128]{2,1,0:T(8,128)(2,1)S(1)}, u32[]{:S(2)}, u32[]{:S(2)}) async-start(bf16[16,176,128]{2,1,0:T(8,128)(2,1)} %get-tuple-element.130), calls=%async_computation.2 | async-start | bytes 1441792 | tf_op jit(solution)/shard_map/all_to_all | solution.py:920
  62.0 10.7 %shard_map.209 = (bf16[90,16,128]{2,1,0:T(8,128)(2,1)}, f32[144,128]{1,0:T(8,128)}, f32[144,128]{1,0:T(8,128)}, bf16[8,144,512]{2,1,0:T(8,128)(2,1)}, bf16[128,1...) custom-call(s32[7]{0:T(128)} %bitcast.21, bf16[384,128]{1,0:T(8,128)(2,1)} %get-tuple-element.116.refs_1_, ...), custom_call_target="tpu_custom_call" | custom-call | flops 8000000000 | bytes 1000000 | tf_op jit(solution)/shard_map/pallas_call | solution.py:902
  72.7 0.3 collective-permute-start.3
  73.0 2.2 %collective-permute-done.3.refs_1_ = bf16[16,176,128]{2,1,0:T(8,128)(2,1)S(1)} collective-permute-done((bf16[16,176,128]{2,1,0:T(8,128)(2,1)S(1)}, bf16[16,176,128]{2,1,0:T(8,128)(2,1)S(1)}, u32[]{:S(2)}, u32[]{:S(2)}) %collective-permute-start.3) | collective-permute-done | bytes 720928 | tf_op jit(solution)/shard_map/ppermute | solution.py:915
  75.2 9.8 %shard_map.210 = (bf16[16,176,128]{2,1,0:T(8,128)(2,1)}, bf16[176,128]{1,0:T(8,128)(2,1)}, f32[144,128]{1,0:T(8,128)}, bf16[432,128]{1,0:T(8,128)(2,1)}, f32[144...) custom-call(bf16[16,176,128]{2,1,0:T(8,128)(2,1)S(1)} %all-to-all-do, ...), custom_call_target="tpu_custom_call" | custom-call | tf_op jit(solution)/shard_map/pallas_call | solution.py:902
  85.0 6.7 %all-to-all-start.3 = ((bf16[16,176,128]{2,1,0:T(8,128)(2,1)}), bf16[16,176,128]{2,1,0:T(8,128)(2,1)S(1)}, u32[]{:S(2)}, u32[]{:S(2)}) async-start(bf16[16,176,128]{2,1,0:T(8,128)(2,1)} %get-tuple-element.156), calls=%async_computation.3 | async-start | bytes 1441792 | tf_op jit(solution)/shard_map/all_to_all | solution.py:920
  91.7 10.8 %shard_map.211 = (bf16[103,16,128]{2,1,0:T(8,128)(2,1)}, bf16[103,16,128]{2,1,0:T(8,128)(2,1)}, bf16[1,16,128]{2,1,0:T(8,128)(2,1)}, f32[144,128]{1,0:T(8,128)},...) custom-call(s32[7]{0:T(128)} %bitcast.23, ...), custom_call_target="tpu_custom_call" | custom-call | flops 8000000000 | bytes 1000000 | tf_op jit(solution)/shard_map/pallas_call | solution.py:902
  102.5 0.5 collective-permute-start.4
  103.0 1.7 %collective-permute-done.5.refs_1_ = bf16[16,176,128]{2,1,0:T(8,128)(2,1)S(1)} collective-permute-done((bf16[16,176,128]{2,1,0:T(8,128)(2,1)S(1)}, bf16[16,176,128]{2,1,0:T(8,128)(2,1)S(1)}, u32[]{:S(2)}, u32[]{:S(2)}) %collective-permute-start.5) | collective-permute-done | bytes 720928 | tf_op jit(solution)/shard_map/ppermute | solution.py:915
  104.7 8.9 %shard_map.212 = (bf16[24,16,128]{2,1,0:T(8,128)(2,1)S(1)}, bf16[24,16,128]{2,1,0:T(8,128)(2,1)S(1)}) custom-call(bf16[16,176,128]{2,1,0:T(8,128)(2,1)S(1)} %all-to-all-done.3.refs_0_, bf16[16,176,128]{2,1,0:T(8,128)(2,1)S(1)} %collective-permute-done.5.refs_1_, s32[7]{0:T(128)} %bitcast.24, f32[7]{0:T(128)} %bitcast.26, s32[7]{0:T(128)} %bitcast.27, ...), custom_call_target="tpu_custom_call" | custom-call | tf_op jit(solution)/shard_map/pallas_call | solution.py:902
  113.6 0.2 collective-permute-start.6
  113.8 1.2 collective-permute-done.6.refs_3_
  115.1 19.7 %all_to_all.30.refs_0_ = bf16[64,40,128]{2,1,0:T(8,128)(2,1)S(1)} all-to-all(bf16[64,40,128]{2,1,0:T(8,128)(2,1)S(1)} %shard_map.213), channel_id=1, replica_groups={{0,2,4,6,8,10,12,14,16,18,20,22,24,26,28,30,32,34,36,38,40,42,44,46,48,..., dimensions={0} | all-to-all | bytes 1310720 | tf_op jit(solution)/shard_map/all_to_all | solution.py:1031
  134.8 0.9 shard_map.214
  135.8 10.1 %all-to-all-start.5 = ((bf16[64,32,128]{2,1,0:T(8,128)(2,1)}), bf16[64,32,128]{2,1,0:T(8,128)(2,1)S(1)}, u32[]{:S(2)}, u32[]{:S(2)}) async-start(bf16[64,32,128]{2,1,0:T(8,128)(2,1)} %get-tuple-element.176), calls=%async_computation.5 | async-start | bytes 1048576 | tf_op jit(solution)/shard_map/all_to_all | solution.py:1034
  146.0 1.2 collective-permute-done.7
  147.3 4.6 %collective-permute-start.8 = (f32[144,128]{1,0:T(8,128)S(1)}, f32[144,128]{1,0:T(8,128)S(1)}, u32[]{:S(2)}, u32[]{:S(2)}) collective-permute-start(f32[144,128]{1,0:T(8,128)S(1)} %broadcast_select_fusion), channel_id=1, source_target_pairs={{0,0},{1,31},{2,2},{3,29},{4,4},{5,27},{6,6},{7,25},{8,8},{9,23},{... | collective-permute-start | bytes 221192 | tf_op jit(solution)/shard_map/ppermute | solution.py:926
  151.8 4.2 %collective-permute-done.8.refs_2_ = f32[144,128]{1,0:T(8,128)S(1)} collective-permute-done((f32[144,128]{1,0:T(8,128)S(1)}, f32[144,128]{1,0:T(8,128)S(1)}, u32[]{:S(2)}, u32[]{:S(2)}) %collective-permute-start.8) | collective-permute-done | bytes 73760 | tf_op jit(solution)/shard_map/ppermute | solution.py:926
  156.1 1.8 %collective-permute-done.9.refs_1_ = bf16[64,32,128]{2,1,0:T(8,128)(2,1)S(1)} collective-permute-done((bf16[64,32,128]{2,1,0:T(8,128)(2,1)S(1)}, bf16[64,32,128]{2,1,0:T(8,128)(2,1)S(1)}, u32[]{:S(2)}, u32[]{:S(2)}) %collective-permute-start.9) | collective-permute-done | bytes 524320 | tf_op jit(solution)/shard_map/ppermute | solution.py:915
  157.9 1.5 shard_map.215
  (18 shorter events, 0.5 us)
Async XLA Ops:
  2.1 17.2 %all-to-all-start = ((f32[32,8,128]{2,1,0:T(8,128)}), f32[32,8,128]{2,1,0:T(8,128)S(1)}, u32[]{:S(2)}, u32[]{:S(2)}) async-start(f32[32,8,128]{2,1,0:T(8,128)} %shard_map.205), calls=%async_computation | async-start | bytes 262144 | tf_op jit(solution)/shard_map/all_to_all | solution.py:955
  19.3 16.3 %copy-start.2 = (bf16[144,128]{1,0:T(8,128)(2,1)S(1)}, bf16[144,128]{1,0:T(8,128)(2,1)}, u32[]{:S(2)}) copy-start(bf16[144,128]{1,0:T(8,128)(2,1)} %get-tuple-element.107) | copy-start | bytes 110596
  29.4 15.1 %all-to-all-start.1 = ((bf16[16,144,128]{2,1,0:T(8,128)(2,1)}), bf16[16,144,128]{2,1,0:T(8,128)(2,1)S(1)}, u32[]{:S(2)}, u32[]{:S(2)}) async-start(bf16[16,144,128]{2,1,0:T(8,128)(2,1)} %get-tuple-element.106), calls=%async_computation.1 | async-start | bytes 1179648 | tf_op jit(solution)/shard_map/all_to_all | solution.py:920
  35.7 8.1 %collective-permute-start = (bf16[144,128]{1,0:T(8,128)(2,1)S(1)}, bf16[144,128]{1,0:T(8,128)(2,1)S(1)}, u32[]{:S(2)}, u32[]{:S(2)}) collective-permute-start(bf16[144,128]{1,0:T(8,128)(2,1)S(1)} %copy-done.2), channel_id=1, source_target_pairs={{0,0},{1,31},{2,2},{3,29},{4,4},{5,27},{6,6},{7,25},{8,8},{9,23},{... | collective-permute-start | bytes 110600 | tf_op jit(solution)/shard_map/ppermute | solution.py:926
  44.6 2.2 %collective-permute-start.1 = (bf16[16,144,128]{2,1,0:T(8,128)(2,1)S(1)}, bf16[16,144,128]{2,1,0:T(8,128)(2,1)S(1)}, u32[]{:S(2)}, u32[]{:S(2)}) collective-permute-start(bf16[16,144,128]{2,1,0:T(8,128)(2,1)S(1)} %all-to-all-done.1.refs_0_), channel_id=1, source_target_pairs={{0,1},{1,0},{2,3},{3,2},{4,5},{5,4},{6,7},{7,6},{8,9},{9,8},{10,11... | collective-permute-start | bytes 1769480 | tf_op jit(solution)/shard_map/ppermute | solution.py:915
  45.0 1.7 %collective-permute-start.2 = (bf16[144,128]{1,0:T(8,128)(2,1)S(1)}, bf16[144,128]{1,0:T(8,128)(2,1)S(1)}, u32[]{:S(2)}, u32[]{:S(2)}) collective-permute-start(bf16[144,128]{1,0:T(8,128)(2,1)S(1)} %collective-permute-done.refs_2_), channel_id=1, source_target_pairs={{0,1},{1,0},{2,3},{3,2},{4,5},{5,4},{6,7},{7,6},{8,9},{9,8},{10,11... | collective-permute-start | bytes 110600 | tf_op jit(solution)/shard_map/ppermute | solution.py:915
  55.2 17.5 %all-to-all-start.2 = ((bf16[16,176,128]{2,1,0:T(8,128)(2,1)}), bf16[16,176,128]{2,1,0:T(8,128)(2,1)S(1)}, u32[]{:S(2)}, u32[]{:S(2)}) async-start(bf16[16,176,128]{2,1,0:T(8,128)(2,1)} %get-tuple-element.130), calls=%async_computation.2 | async-start | bytes 1441792 | tf_op jit(solution)/shard_map/all_to_all | solution.py:920
  72.7 2.5 %collective-permute-start.3 = (bf16[16,176,128]{2,1,0:T(8,128)(2,1)S(1)}, bf16[16,176,128]{2,1,0:T(8,128)(2,1)S(1)}, u32[]{:S(2)}, u32[]{:S(2)}) collective-permute-start(bf16[16,176,128]{2,1,0:T(8,128)(2,1)S(1)} %all-to-all-done.2.refs_0_), channel_id=1, source_target_pairs={{0,1},{1,0},{2,3},{3,2},{4,5},{5,4},{6,7},{7,6},{8,9},{9,8},{10,11... | collective-permute-start | bytes 2162696 | tf_op jit(solution)/shard_map/ppermute | solution.py:915
  85.0 17.5 %all-to-all-start.3 = ((bf16[16,176,128]{2,1,0:T(8,128)(2,1)}), bf16[16,176,128]{2,1,0:T(8,128)(2,1)S(1)}, u32[]{:S(2)}, u32[]{:S(2)}) async-start(bf16[16,176,128]{2,1,0:T(8,128)(2,1)} %get-tuple-element.156), calls=%async_computation.3 | async-start | bytes 1441792 | tf_op jit(solution)/shard_map/all_to_all | solution.py:920
  102.5 2.3 %collective-permute-start.5 = (bf16[16,176,128]{2,1,0:T(8,128)(2,1)S(1)}, bf16[16,176,128]{2,1,0:T(8,128)(2,1)S(1)}, u32[]{:S(2)}, u32[]{:S(2)}) collective-permute-start(bf16[16,176,128]{2,1,0:T(8,128)(2,1)S(1)} %all-to-all-done.3.refs_0_), channel_id=1, source_target_pairs={{0,1},{1,0},{2,3},{3,2},{4,5},{5,4},{6,7},{7,6},{8,9},{9,8},{10,11... | collective-permute-start | bytes 2162696 | tf_op jit(solution)/shard_map/ppermute | solution.py:915
  102.5 11.3 %collective-permute-start.4 = (bf16[103,16,128]{2,1,0:T(8,128)(2,1)}, bf16[103,16,128]{2,1,0:T(8,128)(2,1)S(1)}, u32[]{:S(2)}, u32[]{:S(2)}) collective-permute-start(bf16[103,16,128]{2,1,0:T(8,128)(2,1)} %get-tuple-element.159), channel_id=1, source_target_pairs={{0,1},{1,0},{2,3},{3,2},{4,5},{5,4},{6,7},{7,6},{8,9},{9,8},{10,11... | collective-permute-start | bytes 1265672 | tf_op jit(solution)/shard_map/ppermute | solution.py:915
  104.7 10.3 %copy-start = (bf16[103,16,128]{2,1,0:T(8,128)(2,1)S(1)}, bf16[103,16,128]{2,1,0:T(8,128)(2,1)}, u32[]{:S(2)}) copy-start(bf16[103,16,128]{2,1,0:T(8,128)(2,1)} %get-tuple-element.155.refs_0_) | copy-start | bytes 1265668
  113.6 1.4 collective-permute-start.6
  134.8 11.1 %copy-start.1 = (f32[144,128]{1,0:T(8,128)S(1)}, f32[144,128]{1,0:T(8,128)}, u32[]{:S(2)}) copy-start(f32[144,128]{1,0:T(8,128)} %get-tuple-element.177) | copy-start | bytes 221188
  135.8 20.2 %all-to-all-start.5 = ((bf16[64,32,128]{2,1,0:T(8,128)(2,1)}), bf16[64,32,128]{2,1,0:T(8,128)(2,1)S(1)}, u32[]{:S(2)}, u32[]{:S(2)}) async-start(bf16[64,32,128]{2,1,0:T(8,128)(2,1)} %get-tuple-element.176), calls=%async_computation.5 | async-start | bytes 1048576 | tf_op jit(solution)/shard_map/all_to_all | solution.py:1034
  145.9 1.3 collective-permute-start.7
  147.3 8.7 %collective-permute-start.8 = (f32[144,128]{1,0:T(8,128)S(1)}, f32[144,128]{1,0:T(8,128)S(1)}, u32[]{:S(2)}, u32[]{:S(2)}) collective-permute-start(f32[144,128]{1,0:T(8,128)S(1)} %broadcast_select_fusion), channel_id=1, source_target_pairs={{0,0},{1,31},{2,2},{3,29},{4,4},{5,27},{6,6},{7,25},{8,8},{9,23},{... | collective-permute-start | bytes 221192 | tf_op jit(solution)/shard_map/ppermute | solution.py:926
  156.0 1.9 %collective-permute-start.9 = (bf16[64,32,128]{2,1,0:T(8,128)(2,1)S(1)}, bf16[64,32,128]{2,1,0:T(8,128)(2,1)S(1)}, u32[]{:S(2)}, u32[]{:S(2)}) collective-permute-start(bf16[64,32,128]{2,1,0:T(8,128)(2,1)S(1)} %all-to-all-done.5.refs_0_), channel_id=1, source_target_pairs={{0,1},{1,0},{2,3},{3,2},{4,5},{5,4},{6,7},{7,6},{8,9},{9,8},{10,11... | collective-permute-start | bytes 1572872 | tf_op jit(solution)/shard_map/ppermute | solution.py:915

commit v2 on v1

--- a/solution.py
+++ b/solution.py
@@ -744,7 +744,7 @@
     zero = jnp.zeros((16, TILE), bf16)
     late = late_ref.shape[0] - 1
     series, core = lax.axis_index("series"), lax.axis_index("tm") % 2
-    out_ref[:, 32:40, :] = jnp.zeros((64, 8, TILE), bf16)
+    out_ref[:, 32:48, :] = jnp.zeros((64, 16, TILE), bf16)
 
     def both(ref, in_ref, t):
         return ref[t].astype(f32) + in_ref[t].astype(f32)
@@ -758,9 +758,9 @@
         out_ref[jnp.where(core == 0, t // 2, 63 - t // 2), t % 2 * 16 : t % 2 * 16 + 16, :] = value
     raw = both(late_ref, late_in_ref, late)
     for c in range(16):
-        line = jnp.where(iota((8, 1), 0) == 0, raw[c : c + 1], 0.0)
+        line = jnp.where(iota((16, 1), 0) == 0, raw[c : c + 1], 0.0)
         chip = series * 16 + c
-        out_ref[jnp.where(core == 0, chip, 63 - chip), 32:40, :] = line.astype(bf16)
+        out_ref[jnp.where(core == 0, chip, 63 - chip), 32:48, :] = line.astype(bf16)
 
 
 def sum_kernel(in_ref, out_ref, raw_ref):
@@ -1026,7 +1026,7 @@
         tables=(lengths, scales, ids),
         weights=(qall, k_rows, v_rows, dq, grad, resid0, normal_a0, tail0, tail1, rest, w_dense, feats, own_rope, (w_qkv, 0), gains),
     )
-    packed = call(pair_sum_kernel, (early, early_in, late, pair_permute(late_out, 1)), low(64, 40, TILE))
+    packed = call(pair_sum_kernel, (early, early_in, late, pair_permute(late_out, 1)), low(64, 48, TILE))
     same_core = [[2 * chip for chip in range(64)], [127 - 2 * chip for chip in range(64)]]
     parts = lax.all_to_all(packed, ("series", "tm"), 0, 0, axis_index_groups=same_core)
     share, raw_grad = call(sum_kernel, (parts,), [low(64, 32, TILE), shape(1, TILE)])

time: 160 us -> 161 us (level)
  no operation moved by 1% of the time
where the time goes in v2:
time: 161 us
  Pallas kernels  65.6 us (41%)
  starting transfers between devices  47.5 us (30%)
  waiting for transfers between devices  25.6 us (16%)
  blocking collectives  21.1 us (13%)
    pallas_call x11, Pallas kernels, call(): pl.pallas_call(wrapped, out_shape=outs, in_specs=[vmem] * count + [hbm] *...  65.6 us
    all_to_all x1, blocking collectives, body(): lax.all_to_all(packed, ('series', 'tm'), 0, 0, axis_index_groups=same_core)  21.1 us
    all_to_all x3, starting transfers between devices, gather(): own = lax.all_to_all(copies, 'tm', 0, 0, axis_index_groups=groups)  19.7 us
    ppermute x2, waiting for transfers between devices, swap(): lax.ppermute(block, 'tm', [(n, n if n % 2 == 0 else 32 - n) for n in rang...  10.2 us
    all_to_all x1, starting transfers between devices, body(): lax.all_to_all(share, ('series', 'tm'), 0, 0, axis_index_groups=same_core)  10 us
    ppermute x8, waiting for transfers between devices, pair_permute(): return lax.ppermute(x, 'tm', [(i, i ^ bit) for i in range(32)])  9.77 us
    all_to_all x1, starting transfers between devices, body(): lax.all_to_all(call(first_values_kernel, (), shape(32, 8, TILE), tables=(...  9.61 us
    ppermute x2, starting transfers between devices, swap(): lax.ppermute(block, 'tm', [(n, n if n % 2 == 0 else 32 - n) for n in rang...  6.44 us
  transfers between devices with their start and end apart: 15, of which 10 were waited for; matrix products, arithmetic and copies ran while one was open for 0% of the time, Pallas kernels for 21%

profile of v2, /device:TPU:1, one launch (start us, length us, event | category | flops | bytes accessed | tf_op | source)
XLA Modules:
  0.0 160.7 jit_solution(6170573148902798635)
XLA Ops:
  0.6 1.4 shard_map.205
  2.1 9.6 %all-to-all-start = ((f32[32,8,128]{2,1,0:T(8,128)}), f32[32,8,128]{2,1,0:T(8,128)S(1)}, u32[]{:S(2)}, u32[]{:S(2)}) async-start(f32[32,8,128]{2,1,0:T(8,128)} %shard_map.205), calls=%async_computation | async-start | bytes 262144 | tf_op jit(solution)/shard_map/all_to_all | solution.py:955
  11.7 2.9 %shard_map.206 = (bf16[144,400]{1,0:T(8,128)(2,1)}, bf16[432,144]{1,0:T(8,128)(2,1)}, bf16[144,144]{1,0:T(8,128)(2,1)}, bf16[768,144]{1,0:T(8,128)(2,1)}, bf16[4...) custom-call(s32[1,84]{1,0:T(1,128)} %bitcast.33, ...), custom_call_target="tpu_custom_call" | custom-call | flops 3000000000 | bytes 1000000 | tf_op jit(solution)/shard_map/pallas_call | solution.py:902
  14.6 4.8 %all-to-all-done.refs_0_ = f32[32,8,128]{2,1,0:T(8,128)S(1)} async-done(((f32[32,8,128]{2,1,0:T(8,128)}), f32[32,8,128]{2,1,0:T(8,128)S(1)}, u32[]{:S(2)}, u32[]{:S(2)}) %all-to-all-start) | async-done | bytes 131104 | tf_op jit(solution)/shard_map/all_to_all | solution.py:955
  19.3 10.1 %shard_map.207 = (bf16[16,144,128]{2,1,0:T(8,128)(2,1)}, bf16[144,128]{1,0:T(8,128)(2,1)}, f32[144,128]{1,0:T(8,128)}, bf16[8,144,512]{2,1,0:T(8,128)(2,1)}, bf1...) custom-call(f32[32,8,128]{2,1,0:T(8,128)S(1)} %all-to-all-done.refs_, ...), custom_call_target="tpu_custom_call" | custom-call | tf_op jit(solution)/shard_map/pallas_call | solution.py:902
  29.4 6.3 %all-to-all-start.1 = ((bf16[16,144,128]{2,1,0:T(8,128)(2,1)}), bf16[16,144,128]{2,1,0:T(8,128)(2,1)S(1)}, u32[]{:S(2)}, u32[]{:S(2)}) async-start(bf16[16,144,128]{2,1,0:T(8,128)(2,1)} %get-tuple-element.106), calls=%async_computation.1 | async-start | bytes 1179648 | tf_op jit(solution)/shard_map/all_to_all | solution.py:920
  35.7 2.0 %collective-permute-start = (bf16[144,128]{1,0:T(8,128)(2,1)S(1)}, bf16[144,128]{1,0:T(8,128)(2,1)S(1)}, u32[]{:S(2)}, u32[]{:S(2)}) collective-permute-start(bf16[144,128]{1,0:T(8,128)(2,1)S(1)} %copy-done.2), channel_id=1, source_target_pairs={{0,0},{1,31},{2,2},{3,29},{4,4},{5,27},{6,6},{7,25},{8,8},{9,23},{... | collective-permute-start | bytes 110600 | tf_op jit(solution)/shard_map/ppermute | solution.py:926
  37.7 6.0 %collective-permute-done.refs_2_ = bf16[144,128]{1,0:T(8,128)(2,1)S(1)} collective-permute-done((bf16[144,128]{1,0:T(8,128)(2,1)S(1)}, bf16[144,128]{1,0:T(8,128)(2,1)S(1)}, u32[]{:S(2)}, u32[]{:S(2)}) %collective-permute-start) | collective-permute-done | bytes 36896 | tf_op jit(solution)/shard_map/ppermute | solution.py:926
  43.7 0.8 all-to-all-done.1.refs_0_
  44.6 0.5 collective-permute-start.1
  45.1 1.7 %collective-permute-done.2.refs_3_ = bf16[144,128]{1,0:T(8,128)(2,1)S(1)} collective-permute-done((bf16[144,128]{1,0:T(8,128)(2,1)S(1)}, bf16[144,128]{1,0:T(8,128)(2,1)S(1)}, u32[]{:S(2)}, u32[]{:S(2)}) %collective-permute-start.2) | collective-permute-done | bytes 36896 | tf_op jit(solution)/shard_map/ppermute | solution.py:915
  46.7 8.5 %shard_map.208 = (bf16[16,176,128]{2,1,0:T(8,128)(2,1)}, bf16[176,128]{1,0:T(8,128)(2,1)}, f32[144,128]{1,0:T(8,128)}, bf16[8,144,512]{2,1,0:T(8,128)(2,1)}, bf1...) custom-call(bf16[16,144,128]{2,1,0:T(8,128)(2,1)S(1)} %all-to-all-do, ...), custom_call_target="tpu_custom_call" | custom-call | tf_op jit(solution)/shard_map/pallas_call | solution.py:902
  55.2 6.7 %all-to-all-start.2 = ((bf16[16,176,128]{2,1,0:T(8,128)(2,1)}), bf16[16,176,128]{2,1,0:T(8,128)(2,1)S(1)}, u32[]{:S(2)}, u32[]{:S(2)}) async-start(bf16[16,176,128]{2,1,0:T(8,128)(2,1)} %get-tuple-element.130), calls=%async_computation.2 | async-start | bytes 1441792 | tf_op jit(solution)/shard_map/all_to_all | solution.py:920
  62.0 10.7 %shard_map.209 = (bf16[90,16,128]{2,1,0:T(8,128)(2,1)}, f32[144,128]{1,0:T(8,128)}, f32[144,128]{1,0:T(8,128)}, bf16[8,144,512]{2,1,0:T(8,128)(2,1)}, bf16[128,1...) custom-call(s32[7]{0:T(128)} %bitcast.21, bf16[384,128]{1,0:T(8,128)(2,1)} %get-tuple-element.116.refs_1_, ...), custom_call_target="tpu_custom_call" | custom-call | flops 8000000000 | bytes 1000000 | tf_op jit(solution)/shard_map/pallas_call | solution.py:902
  72.7 0.3 collective-permute-start.3
  73.0 2.2 %collective-permute-done.3.refs_1_ = bf16[16,176,128]{2,1,0:T(8,128)(2,1)S(1)} collective-permute-done((bf16[16,176,128]{2,1,0:T(8,128)(2,1)S(1)}, bf16[16,176,128]{2,1,0:T(8,128)(2,1)S(1)}, u32[]{:S(2)}, u32[]{:S(2)}) %collective-permute-start.3) | collective-permute-done | bytes 720928 | tf_op jit(solution)/shard_map/ppermute | solution.py:915
  75.2 9.8 %shard_map.210 = (bf16[16,176,128]{2,1,0:T(8,128)(2,1)}, bf16[176,128]{1,0:T(8,128)(2,1)}, f32[144,128]{1,0:T(8,128)}, bf16[432,128]{1,0:T(8,128)(2,1)}, f32[144...) custom-call(bf16[16,176,128]{2,1,0:T(8,128)(2,1)S(1)} %all-to-all-do, ...), custom_call_target="tpu_custom_call" | custom-call | tf_op jit(solution)/shard_map/pallas_call | solution.py:902
  85.0 6.7 %all-to-all-start.3 = ((bf16[16,176,128]{2,1,0:T(8,128)(2,1)}), bf16[16,176,128]{2,1,0:T(8,128)(2,1)S(1)}, u32[]{:S(2)}, u32[]{:S(2)}) async-start(bf16[16,176,128]{2,1,0:T(8,128)(2,1)} %get-tuple-element.156), calls=%async_computation.3 | async-start | bytes 1441792 | tf_op jit(solution)/shard_map/all_to_all | solution.py:920
  91.7 10.8 %shard_map.211 = (bf16[103,16,128]{2,1,0:T(8,128)(2,1)}, bf16[103,16,128]{2,1,0:T(8,128)(2,1)}, bf16[1,16,128]{2,1,0:T(8,128)(2,1)}, f32[144,128]{1,0:T(8,128)},...) custom-call(s32[7]{0:T(128)} %bitcast.23, ...), custom_call_target="tpu_custom_call" | custom-call | flops 8000000000 | bytes 1000000 | tf_op jit(solution)/shard_map/pallas_call | solution.py:902
  102.5 0.5 collective-permute-start.4
  103.0 1.7 %collective-permute-done.5.refs_1_ = bf16[16,176,128]{2,1,0:T(8,128)(2,1)S(1)} collective-permute-done((bf16[16,176,128]{2,1,0:T(8,128)(2,1)S(1)}, bf16[16,176,128]{2,1,0:T(8,128)(2,1)S(1)}, u32[]{:S(2)}, u32[]{:S(2)}) %collective-permute-start.5) | collective-permute-done | bytes 720928 | tf_op jit(solution)/shard_map/ppermute | solution.py:915
  104.7 8.9 %shard_map.212 = (bf16[24,16,128]{2,1,0:T(8,128)(2,1)S(1)}, bf16[24,16,128]{2,1,0:T(8,128)(2,1)S(1)}) custom-call(bf16[16,176,128]{2,1,0:T(8,128)(2,1)S(1)} %all-to-all-done.3.refs_0_, bf16[16,176,128]{2,1,0:T(8,128)(2,1)S(1)} %collective-permute-done.5.refs_1_, s32[7]{0:T(128)} %bitcast.24, f32[7]{0:T(128)} %bitcast.26, s32[7]{0:T(128)} %bitcast.27, ...), custom_call_target="tpu_custom_call" | custom-call | tf_op jit(solution)/shard_map/pallas_call | solution.py:902
  113.6 0.2 collective-permute-start.6
  113.8 1.2 collective-permute-done.6.refs_3_
  115.2 21.1 %all_to_all.30.refs_0_ = bf16[64,48,128]{2,1,0:T(8,128)(2,1)S(1)} all-to-all(bf16[64,48,128]{2,1,0:T(8,128)(2,1)S(1)} %shard_map.213), channel_id=1, replica_groups={{0,2,4,6,8,10,12,14,16,18,20,22,24,26,28,30,32,34,36,38,40,42,44,46,48,..., dimensions={0} | all-to-all | bytes 1572864 | tf_op jit(solution)/shard_map/all_to_all | solution.py:1031
  136.3 0.9 shard_map.214
  137.2 10.0 %all-to-all-start.5 = ((bf16[64,32,128]{2,1,0:T(8,128)(2,1)}), bf16[64,32,128]{2,1,0:T(8,128)(2,1)S(1)}, u32[]{:S(2)}, u32[]{:S(2)}) async-start(bf16[64,32,128]{2,1,0:T(8,128)(2,1)} %get-tuple-element.176), calls=%async_computation.5 | async-start | bytes 1048576 | tf_op jit(solution)/shard_map/all_to_all | solution.py:1034
  147.4 1.2 collective-permute-done.7
  148.6 4.4 %collective-permute-start.8 = (f32[144,128]{1,0:T(8,128)S(1)}, f32[144,128]{1,0:T(8,128)S(1)}, u32[]{:S(2)}, u32[]{:S(2)}) collective-permute-start(f32[144,128]{1,0:T(8,128)S(1)} %broadcast_select_fusion), channel_id=1, source_target_pairs={{0,0},{1,31},{2,2},{3,29},{4,4},{5,27},{6,6},{7,25},{8,8},{9,23},{... | collective-permute-start | bytes 221192 | tf_op jit(solution)/shard_map/ppermute | solution.py:926
  153.1 4.2 %collective-permute-done.8.refs_2_ = f32[144,128]{1,0:T(8,128)S(1)} collective-permute-done((f32[144,128]{1,0:T(8,128)S(1)}, f32[144,128]{1,0:T(8,128)S(1)}, u32[]{:S(2)}, u32[]{:S(2)}) %collective-permute-start.8) | collective-permute-done | bytes 73760 | tf_op jit(solution)/shard_map/ppermute | solution.py:926
  157.3 1.9 %collective-permute-done.9.refs_1_ = bf16[64,32,128]{2,1,0:T(8,128)(2,1)S(1)} collective-permute-done((bf16[64,32,128]{2,1,0:T(8,128)(2,1)S(1)}, bf16[64,32,128]{2,1,0:T(8,128)(2,1)S(1)}, u32[]{:S(2)}, u32[]{:S(2)}) %collective-permute-start.9) | collective-permute-done | bytes 524320 | tf_op jit(solution)/shard_map/ppermute | solution.py:915
  159.1 1.5 shard_map.215
  (18 shorter events, 0.5 us)
Async XLA Ops:
  2.1 17.2 %all-to-all-start = ((f32[32,8,128]{2,1,0:T(8,128)}), f32[32,8,128]{2,1,0:T(8,128)S(1)}, u32[]{:S(2)}, u32[]{:S(2)}) async-start(f32[32,8,128]{2,1,0:T(8,128)} %shard_map.205), calls=%async_computation | async-start | bytes 262144 | tf_op jit(solution)/shard_map/all_to_all | solution.py:955
  19.3 16.3 %copy-start.2 = (bf16[144,128]{1,0:T(8,128)(2,1)S(1)}, bf16[144,128]{1,0:T(8,128)(2,1)}, u32[]{:S(2)}) copy-start(bf16[144,128]{1,0:T(8,128)(2,1)} %get-tuple-element.107) | copy-start | bytes 110596
  29.4 15.1 %all-to-all-start.1 = ((bf16[16,144,128]{2,1,0:T(8,128)(2,1)}), bf16[16,144,128]{2,1,0:T(8,128)(2,1)S(1)}, u32[]{:S(2)}, u32[]{:S(2)}) async-start(bf16[16,144,128]{2,1,0:T(8,128)(2,1)} %get-tuple-element.106), calls=%async_computation.1 | async-start | bytes 1179648 | tf_op jit(solution)/shard_map/all_to_all | solution.py:920
  35.7 8.1 %collective-permute-start = (bf16[144,128]{1,0:T(8,128)(2,1)S(1)}, bf16[144,128]{1,0:T(8,128)(2,1)S(1)}, u32[]{:S(2)}, u32[]{:S(2)}) collective-permute-start(bf16[144,128]{1,0:T(8,128)(2,1)S(1)} %copy-done.2), channel_id=1, source_target_pairs={{0,0},{1,31},{2,2},{3,29},{4,4},{5,27},{6,6},{7,25},{8,8},{9,23},{... | collective-permute-start | bytes 110600 | tf_op jit(solution)/shard_map/ppermute | solution.py:926
  44.6 2.2 %collective-permute-start.1 = (bf16[16,144,128]{2,1,0:T(8,128)(2,1)S(1)}, bf16[16,144,128]{2,1,0:T(8,128)(2,1)S(1)}, u32[]{:S(2)}, u32[]{:S(2)}) collective-permute-start(bf16[16,144,128]{2,1,0:T(8,128)(2,1)S(1)} %all-to-all-done.1.refs_0_), channel_id=1, source_target_pairs={{0,1},{1,0},{2,3},{3,2},{4,5},{5,4},{6,7},{7,6},{8,9},{9,8},{10,11... | collective-permute-start | bytes 1769480 | tf_op jit(solution)/shard_map/ppermute | solution.py:915
  45.0 1.7 %collective-permute-start.2 = (bf16[144,128]{1,0:T(8,128)(2,1)S(1)}, bf16[144,128]{1,0:T(8,128)(2,1)S(1)}, u32[]{:S(2)}, u32[]{:S(2)}) collective-permute-start(bf16[144,128]{1,0:T(8,128)(2,1)S(1)} %collective-permute-done.refs_2_), channel_id=1, source_target_pairs={{0,1},{1,0},{2,3},{3,2},{4,5},{5,4},{6,7},{7,6},{8,9},{9,8},{10,11... | collective-permute-start | bytes 110600 | tf_op jit(solution)/shard_map/ppermute | solution.py:915
  55.2 17.5 %all-to-all-start.2 = ((bf16[16,176,128]{2,1,0:T(8,128)(2,1)}), bf16[16,176,128]{2,1,0:T(8,128)(2,1)S(1)}, u32[]{:S(2)}, u32[]{:S(2)}) async-start(bf16[16,176,128]{2,1,0:T(8,128)(2,1)} %get-tuple-element.130), calls=%async_computation.2 | async-start | bytes 1441792 | tf_op jit(solution)/shard_map/all_to_all | solution.py:920
  72.7 2.5 %collective-permute-start.3 = (bf16[16,176,128]{2,1,0:T(8,128)(2,1)S(1)}, bf16[16,176,128]{2,1,0:T(8,128)(2,1)S(1)}, u32[]{:S(2)}, u32[]{:S(2)}) collective-permute-start(bf16[16,176,128]{2,1,0:T(8,128)(2,1)S(1)} %all-to-all-done.2.refs_0_), channel_id=1, source_target_pairs={{0,1},{1,0},{2,3},{3,2},{4,5},{5,4},{6,7},{7,6},{8,9},{9,8},{10,11... | collective-permute-start | bytes 2162696 | tf_op jit(solution)/shard_map/ppermute | solution.py:915
  85.0 17.5 %all-to-all-start.3 = ((bf16[16,176,128]{2,1,0:T(8,128)(2,1)}), bf16[16,176,128]{2,1,0:T(8,128)(2,1)S(1)}, u32[]{:S(2)}, u32[]{:S(2)}) async-start(bf16[16,176,128]{2,1,0:T(8,128)(2,1)} %get-tuple-element.156), calls=%async_computation.3 | async-start | bytes 1441792 | tf_op jit(solution)/shard_map/all_to_all | solution.py:920
  102.5 2.3 %collective-permute-start.5 = (bf16[16,176,128]{2,1,0:T(8,128)(2,1)S(1)}, bf16[16,176,128]{2,1,0:T(8,128)(2,1)S(1)}, u32[]{:S(2)}, u32[]{:S(2)}) collective-permute-start(bf16[16,176,128]{2,1,0:T(8,128)(2,1)S(1)} %all-to-all-done.3.refs_0_), channel_id=1, source_target_pairs={{0,1},{1,0},{2,3},{3,2},{4,5},{5,4},{6,7},{7,6},{8,9},{9,8},{10,11... | collective-permute-start | bytes 2162696 | tf_op jit(solution)/shard_map/ppermute | solution.py:915
  102.5 11.3 %collective-permute-start.4 = (bf16[103,16,128]{2,1,0:T(8,128)(2,1)}, bf16[103,16,128]{2,1,0:T(8,128)(2,1)S(1)}, u32[]{:S(2)}, u32[]{:S(2)}) collective-permute-start(bf16[103,16,128]{2,1,0:T(8,128)(2,1)} %get-tuple-element.159), channel_id=1, source_target_pairs={{0,1},{1,0},{2,3},{3,2},{4,5},{5,4},{6,7},{7,6},{8,9},{9,8},{10,11... | collective-permute-start | bytes 1265672 | tf_op jit(solution)/shard_map/ppermute | solution.py:915
  104.7 10.3 %copy-start = (bf16[103,16,128]{2,1,0:T(8,128)(2,1)S(1)}, bf16[103,16,128]{2,1,0:T(8,128)(2,1)}, u32[]{:S(2)}) copy-start(bf16[103,16,128]{2,1,0:T(8,128)(2,1)} %get-tuple-element.155.refs_0_) | copy-start | bytes 1265668
  113.6 1.4 collective-permute-start.6
  136.3 11.0 %copy-start.1 = (f32[144,128]{1,0:T(8,128)S(1)}, f32[144,128]{1,0:T(8,128)}, u32[]{:S(2)}) copy-start(f32[144,128]{1,0:T(8,128)} %get-tuple-element.177) | copy-start | bytes 221188
  137.2 20.0 %all-to-all-start.5 = ((bf16[64,32,128]{2,1,0:T(8,128)(2,1)}), bf16[64,32,128]{2,1,0:T(8,128)(2,1)S(1)}, u32[]{:S(2)}, u32[]{:S(2)}) async-start(bf16[64,32,128]{2,1,0:T(8,128)(2,1)} %get-tuple-element.176), calls=%async_computation.5 | async-start | bytes 1048576 | tf_op jit(solution)/shard_map/all_to_all | solution.py:1034
  147.3 1.3 collective-permute-start.7
  148.6 8.6 %collective-permute-start.8 = (f32[144,128]{1,0:T(8,128)S(1)}, f32[144,128]{1,0:T(8,128)S(1)}, u32[]{:S(2)}, u32[]{:S(2)}) collective-permute-start(f32[144,128]{1,0:T(8,128)S(1)} %broadcast_select_fusion), channel_id=1, source_target_pairs={{0,0},{1,31},{2,2},{3,29},{4,4},{5,27},{6,6},{7,25},{8,8},{9,23},{... | collective-permute-start | bytes 221192 | tf_op jit(solution)/shard_map/ppermute | solution.py:926
  157.2 1.9 %collective-permute-start.9 = (bf16[64,32,128]{2,1,0:T(8,128)(2,1)S(1)}, bf16[64,32,128]{2,1,0:T(8,128)(2,1)S(1)}, u32[]{:S(2)}, u32[]{:S(2)}) collective-permute-start(bf16[64,32,128]{2,1,0:T(8,128)(2,1)S(1)} %all-to-all-done.5.refs_0_), channel_id=1, source_target_pairs={{0,1},{1,0},{2,3},{3,2},{4,5},{5,4},{6,7},{7,6},{8,9},{9,8},{10,11... | collective-permute-start | bytes 1572872 | tf_op jit(solution)/shard_map/ppermute | solution.py:915
